TPU v7x, 32 devices: a whole 2x2x4 slice. The times are simulated.
32 devices in a mesh: dp: 32 (over z, y, x, core).
Axes of the slice: x: 2, y: 2, z: 4, core: 2. Of those that a mesh axis runs over, the one named last changes fastest.
Arguments:
- hidden_in: bfloat16 [2048, 4096], P('dp'), may hold values from -6 to 6
- queries: bfloat16 [2048, 2048], P('dp'), may hold values from -16 to 16
- keys: bfloat16 [2048, 512], P('dp'), may hold values from -16 to 16
- values: bfloat16 [2048, 512], P('dp'), may hold values from -6 to 6
- grad_attn: bfloat16 [2048, 2048], P('dp'), may hold values from -6 to 6
- send_rows: int32 [4, 32], replicated, may hold values from -1 to 63, as said below
- slot_docs: int32 [32, 4], P('dp'), may hold values from -1 to 63, as said below
Outputs:
- grad_queries: bfloat16 [2048, 2048], P('dp')
- grad_keys: bfloat16 [2048, 512], P('dp')
- grad_values: bfloat16 [2048, 512], P('dp')
- grad_wv: float32 [4096, 512], P('dp')
Inputs may be any that keep to these rules, and one draw needn't show every extreme that they name: `send_rows`: every owner sends the same local rows to a rank. Each local row appears exactly once. The rows sent to one rank form whole documents at consecutive slots, the local rows of a document consecutive and rising with the slot; a document has at most 4 local rows, and in every draw some rank has all 4 slots used. slot_docs[r, j] is -1 exactly where send_rows[j, r] is -1; slots with the same number hold one document, and distinct documents have distinct numbers.
All inputs are finite; a program needn't handle non-finite values.
Results may differ from a plain program's by a relative error of at most 0.0057.
Values may be sent and summed in bfloat16 or wider, within the bound.
A program may use at most 128 MiB of HBM per device.

v0:
```python
import math

import jax
import jax.numpy as jnp
from jax import lax
from jax.sharding import PartitionSpec as P

HQ = 16
HK = 4
DH = 128


def attend_rows(q_rows, k_rows, v_rows, o_rows, segment):
    row_count = q_rows.shape[0]
    group_size = HQ // HK
    score_scale = 1.0 / math.sqrt(DH)
    order_ids = jnp.arange(row_count, dtype=jnp.int32)
    live_rows = segment >= 0
    allowed = (
        (segment[:, None] == segment[None, :])
        & (order_ids[None, :] <= order_ids[:, None])
        & live_rows[:, None]
    )
    q_four = q_rows.reshape(row_count, HK, group_size, DH)
    o_four = o_rows.reshape(row_count, HK, group_size, DH)
    k_three = k_rows.reshape(row_count, HK, DH)
    v_three = v_rows.reshape(row_count, HK, DH)
    grad_q_list = []
    grad_k_list = []
    grad_v_list = []
    for head_kv in range(HK):
        q_group = q_four[:, head_kv]
        o_group = o_four[:, head_kv]
        k_group = k_three[:, head_kv]
        v_group = v_three[:, head_kv]
        scores = (
            jnp.einsum("qhd,kd->hqk", q_group, k_group, preferred_element_type=jnp.float32)
            * score_scale
        )
        scores = jnp.where(allowed[None], scores, jnp.float32(-1000000000.0))
        row_max = jnp.max(scores, axis=-1, keepdims=True)
        weights = jnp.exp(scores - row_max)
        attn_probs = weights / jnp.sum(weights, axis=-1, keepdims=True)
        attn_probs = jnp.where(live_rows[None, :, None], attn_probs, jnp.float32(0.0))
        probs_b = attn_probs.astype(jnp.bfloat16)
        grad_v_list.append(
            jnp.einsum("hqk,qhd->kd", probs_b, o_group, preferred_element_type=jnp.float32)
        )
        dprob = jnp.einsum("qhd,kd->hqk", o_group, v_group, preferred_element_type=jnp.float32)
        row_delta = jnp.sum(attn_probs * dprob, axis=-1, keepdims=True)
        dscore = (attn_probs * (dprob - row_delta) * score_scale).astype(jnp.bfloat16)
        grad_q_list.append(
            jnp.einsum("hqk,kd->qhd", dscore, k_group, preferred_element_type=jnp.float32)
        )
        grad_k_list.append(
            jnp.einsum("hqk,qhd->kd", dscore, q_group, preferred_element_type=jnp.float32)
        )
    grad_q_rows = jnp.stack(grad_q_list, axis=1).reshape(row_count, HQ * DH).astype(jnp.bfloat16)
    grad_k_rows = jnp.stack(grad_k_list, axis=1).reshape(row_count, HK * DH).astype(jnp.bfloat16)
    grad_v_rows = jnp.stack(grad_v_list, axis=1).reshape(row_count, HK * DH).astype(jnp.bfloat16)
    return (grad_q_rows, grad_k_rows, grad_v_rows)


def local(hidden_in, queries, keys, values, grad_attn, send_rows, slot_docs):
    owners = lax.axis_size("dp")
    slot_count = send_rows.shape[0]
    tok_rows = queries.shape[0]
    live_send = send_rows >= 0
    pick_rows = jnp.maximum(send_rows, 0)
    grad_scale = 1.0 / math.sqrt(tok_rows * owners)

    def pack_rows(table):
        return jnp.where(live_send[:, :, None], table[pick_rows], jnp.zeros((), table.dtype))

    def flatten(block):
        return block.reshape(slot_count * owners, block.shape[2])

    def unflatten(block):
        return block.reshape(slot_count, owners, block.shape[1])

    targets = jnp.where(live_send, send_rows, tok_rows).reshape(-1)

    def place_rows(block):
        return (
            jnp.zeros((tok_rows, block.shape[2]), block.dtype)
            .at[targets]
            .set(flatten(block), mode="drop")
        )

    q_in, k_in, v_in, o_in = (
        lax.all_to_all(pack_rows(queries), "dp", split_axis=1, concat_axis=1, tiled=True),
        lax.all_to_all(pack_rows(keys), "dp", split_axis=1, concat_axis=1, tiled=True),
        lax.all_to_all(pack_rows(values), "dp", split_axis=1, concat_axis=1, tiled=True),
        lax.all_to_all(pack_rows(grad_attn), "dp", split_axis=1, concat_axis=1, tiled=True),
    )
    segment = jnp.broadcast_to(slot_docs[0][:, None], (slot_count, owners)).reshape(-1)
    grad_q_rows, grad_k_rows, grad_v_rows = attend_rows(
        flatten(q_in), flatten(k_in), flatten(v_in), flatten(o_in), segment
    )
    q_home, k_home, v_home = (
        lax.all_to_all(unflatten(grad_q_rows), "dp", split_axis=1, concat_axis=1, tiled=True),
        lax.all_to_all(unflatten(grad_k_rows), "dp", split_axis=1, concat_axis=1, tiled=True),
        lax.all_to_all(unflatten(grad_v_rows), "dp", split_axis=1, concat_axis=1, tiled=True),
    )
    grad_queries = place_rows(q_home)
    grad_keys = place_rows(k_home)
    grad_values = place_rows(v_home)
    grad_wv = lax.psum_scatter(
        jnp.einsum("td,tc->dc", hidden_in, grad_values, preferred_element_type=jnp.float32)
        * grad_scale,
        "dp",
        scatter_dimension=0,
        tiled=True,
    )
    return (grad_queries, grad_keys, grad_values, grad_wv)


def solution(mesh):
    placed = (
        P("dp", None),
        P("dp", None),
        P("dp", None),
        P("dp", None),
        P("dp", None),
        P(),
        P("dp", None),
    )
    return jax.shard_map(
        local,
        mesh=mesh,
        in_specs=placed,
        out_specs=(P("dp", None), P("dp", None), P("dp", None), P("dp", None)),
        check_vma=False,
    )
```

profile of v0, /device:TPU:0, one launch (start us, length us, event | category | flops | bytes accessed | tf_op | source)
XLA Modules:
  0.0 244.5 jit_solution(14473836971691566040)
XLA Ops:
  8.8 1.7 gather_fusion.2
  10.6 1.7 gather_fusion
  13.2 7.3 %all-to-all-start = ((bf16[4,32,512]{2,0,1:T(4,128)(2,1)}), bf16[4,32,512]{2,0,1:T(4,128)(2,1)S(1)}, u32[]{:S(2)}, u32[]{:S(2)}) async-start(bf16[4,32,512]{2,0,1:T(4,128)(2,1)} %get-tuple-element.38), calls=%async_computation | async-start | bytes 262144 | tf_op jit(solution)/shard_map/all_to_all | solution.py:92
  20.5 2.4 gather_fusion.3
  23.9 1.7 copy_select_fusion.1
  25.6 3.1 %all-to-all-done = bf16[4,32,512]{2,0,1:T(4,128)(2,1)S(1)} async-done(((bf16[4,32,512]{2,0,1:T(4,128)(2,1)}), bf16[4,32,512]{2,0,1:T(4,128)(2,1)S(1)}, u32[]{:S(2)}, u32[]{:S(2)}) %all-to-all-start) | async-done | bytes 131104 | tf_op jit(solution)/shard_map/all_to_all | solution.py:92
  28.7 18.0 %all_to_all.35 = bf16[4,32,2048]{2,0,1:T(4,128)(2,1)S(1)} all-to-all(bf16[4,32,2048]{2,0,1:T(4,128)(2,1)S(1)} %get-tuple-element.36), channel_id=1, replica_groups=mesh['dp'=32] {'dp'}, dimensions={1} | all-to-all | bytes 1048576 | tf_op jit(solution)/shard_map/all_to_all | solution.py:91
  46.8 3.1 %all-to-all-start.3 = ((bf16[4,32,2048]{2,0,1:T(4,128)(2,1)}), bf16[4,32,2048]{2,0,1:T(4,128)(2,1)S(1)}, u32[]{:S(2)}, u32[]{:S(2)}) async-start(bf16[4,32,2048]{2,0,1:T(4,128)(2,1)} %get-tuple-element.37), calls=%async_computation.3 | async-start | bytes 1048576 | tf_op jit(solution)/shard_map/all_to_all | solution.py:94
  51.2 14.1 %all-to-all-done.3 = bf16[4,32,2048]{2,0,1:T(4,128)(2,1)S(1)} async-done(((bf16[4,32,2048]{2,0,1:T(4,128)(2,1)}), bf16[4,32,2048]{2,0,1:T(4,128)(2,1)S(1)}, u32[]{:S(2)}, u32[]{:S(2)}) %all-to-all-start.3) | async-done | bytes 524320 | tf_op jit(solution)/shard_map/all_to_all | solution.py:94
  69.0 3.1 %all-to-all-start.6 = ((bf16[4,32,512]{2,0,1:T(4,128)(2,1)}), bf16[4,32,512]{2,0,1:T(4,128)(2,1)S(1)}, u32[]{:S(2)}, u32[]{:S(2)}) async-start(bf16[4,32,512]{2,0,1:T(4,128)(2,1)} %copy.131), calls=%async_computation.6 | async-start | bytes 262144 | tf_op jit(solution)/shard_map/all_to_all | solution.py:103
  72.2 8.1 %all-to-all-done.6 = bf16[4,32,512]{2,0,1:T(4,128)(2,1)S(1)} async-done(((bf16[4,32,512]{2,0,1:T(4,128)(2,1)}), bf16[4,32,512]{2,0,1:T(4,128)(2,1)S(1)}, u32[]{:S(2)}, u32[]{:S(2)}) %all-to-all-start.6) | async-done | bytes 131104 | tf_op jit(solution)/shard_map/all_to_all | solution.py:103
  80.3 1.1 scatter_custom_fusion.2
  81.4 4.5 %multiply_bitcast_fusion = f32[4096,512]{0,1:T(8,128)} fusion(bf16[64,512]{1,0:T(8,128)(2,1)S(1)} %scatter_custom_fusion.2, bf16[64,4096]{1,0:T(8,128)(2,1)S(1)} %copy-done), kind=kOutput, calls=%fused_computation.15 | convolution fusion | flops 270532608 | bytes 8978432 | tf_op jit(solution)/shard_map/td,tc->dc/dot_general | solution.py:109
  85.9 10.5 %all_to_all.36 = bf16[4,32,512]{2,0,1:T(4,128)(2,1)S(1)} all-to-all(bf16[4,32,512]{2,0,1:T(4,128)(2,1)S(1)} %get-tuple-element.39), channel_id=1, replica_groups=mesh['dp'=32] {'dp'}, dimensions={1} | all-to-all | bytes 262144 | tf_op jit(solution)/shard_map/all_to_all | solution.py:93
  99.4 2.8 %all-to-all-start.5 = ((bf16[4,32,512]{2,0,1:T(4,128)(2,1)}), bf16[4,32,512]{2,0,1:T(4,128)(2,1)S(1)}, u32[]{:S(2)}, u32[]{:S(2)}) async-start(bf16[4,32,512]{2,0,1:T(4,128)(2,1)} %copy.128), calls=%async_computation.5 | async-start | bytes 262144 | tf_op jit(solution)/shard_map/all_to_all | solution.py:102
  102.2 1.3 fusion.40
  105.1 1.3 copy.125
  106.4 4.6 %all-to-all-done.5 = bf16[4,32,512]{2,0,1:T(4,128)(2,1)S(1)} async-done(((bf16[4,32,512]{2,0,1:T(4,128)(2,1)}), bf16[4,32,512]{2,0,1:T(4,128)(2,1)S(1)}, u32[]{:S(2)}, u32[]{:S(2)}) %all-to-all-start.5) | async-done | bytes 131104 | tf_op jit(solution)/shard_map/all_to_all | solution.py:102
  110.9 2.6 %all-to-all-start.4 = ((bf16[4,32,2048]{2,0,1:T(4,128)(2,1)}), bf16[4,32,2048]{2,0,1:T(4,128)(2,1)S(1)}, u32[]{:S(2)}, u32[]{:S(2)}) async-start(bf16[4,32,2048]{2,0,1:T(4,128)(2,1)} %copy.125), calls=%async_computation.4 | async-start | bytes 1048576 | tf_op jit(solution)/shard_map/all_to_all | solution.py:101
  113.6 1.6 scatter_custom_fusion.1
  115.2 16.7 %all-to-all-done.4 = bf16[4,32,2048]{2,0,1:T(4,128)(2,1)S(1)} async-done(((bf16[4,32,2048]{2,0,1:T(4,128)(2,1)}), bf16[4,32,2048]{2,0,1:T(4,128)(2,1)S(1)}, u32[]{:S(2)}, u32[]{:S(2)}) %all-to-all-start.4) | async-done | bytes 524320 | tf_op jit(solution)/shard_map/all_to_all | solution.py:101
  132.2 2.0 scatter_custom_fusion
  134.2 101.7 %reduce-scatter.2.cloned.1.call-done = f32[128,512]{0,1:T(8,128)} async-done(((f32[4096,512]{0,1:T(8,128)}), f32[128,512]{0,1:T(8,128)}) %reduce-scatter.2.cloned.1.call-update) | async-done | bytes 262160 | tf_op jit(solution)/shard_map/reduce_scatter | solution.py:108
  235.9 1.8 copy.133
  (70 shorter events, 13.4 us)
Async XLA Ops:
  7.2 74.2 %copy-start = (bf16[64,4096]{1,0:T(8,128)(2,1)S(1)}, bf16[64,4096]{1,0:T(8,128)(2,1)}, u32[]{:S(2)}) copy-start(bf16[64,4096]{1,0:T(8,128)(2,1)} %param.7) | copy-start | bytes 1572868
  7.2 15.8 %copy-start.1 = (bf16[64,2048]{1,0:T(8,128)(2,1)S(1)}, bf16[64,2048]{1,0:T(8,128)(2,1)}, u32[]{:S(2)}) copy-start(bf16[64,2048]{1,0:T(8,128)(2,1)} %param.8) | copy-start | bytes 786436
  8.8 41.0 %copy-start.3 = (s32[1,4]{1,0:T(1,128)S(1)}, s32[1,4]{1,0:T(1,128)}, u32[]{:S(2)}) copy-start(s32[1,4]{1,0:T(1,128)} %param.13) | copy-start | bytes 52
  13.2 15.5 %all-to-all-start = ((bf16[4,32,512]{2,0,1:T(4,128)(2,1)}), bf16[4,32,512]{2,0,1:T(4,128)(2,1)S(1)}, u32[]{:S(2)}, u32[]{:S(2)}) async-start(bf16[4,32,512]{2,0,1:T(4,128)(2,1)} %get-tuple-element.38), calls=%async_computation | async-start | bytes 262144 | tf_op jit(solution)/shard_map/all_to_all | solution.py:92
  46.8 18.6 %all-to-all-start.3 = ((bf16[4,32,2048]{2,0,1:T(4,128)(2,1)}), bf16[4,32,2048]{2,0,1:T(4,128)(2,1)S(1)}, u32[]{:S(2)}, u32[]{:S(2)}) async-start(bf16[4,32,2048]{2,0,1:T(4,128)(2,1)} %get-tuple-element.37), calls=%async_computation.3 | async-start | bytes 1048576 | tf_op jit(solution)/shard_map/all_to_all | solution.py:94
  66.5 30.4 %copy-start.4 = (f32[4,128,128]{1,2,0:T(8,128)}, f32[4,128,128]{1,2,0:T(8,128)S(1)}, u32[]{:S(2)}) copy-start(f32[4,128,128]{1,2,0:T(8,128)S(1)} %get-tuple-element.49) | copy-start | bytes 786436
  69.0 11.3 %all-to-all-start.6 = ((bf16[4,32,512]{2,0,1:T(4,128)(2,1)}), bf16[4,32,512]{2,0,1:T(4,128)(2,1)S(1)}, u32[]{:S(2)}, u32[]{:S(2)}) async-start(bf16[4,32,512]{2,0,1:T(4,128)(2,1)} %copy.131), calls=%async_computation.6 | async-start | bytes 262144 | tf_op jit(solution)/shard_map/all_to_all | solution.py:103
  72.1 163.8 %reduce-scatter.2.cloned.1.call-start = ((), (), s32[]{:S(2)}) async-start(), calls=%async_computation.8 | async-start | bytes 8650752 | tf_op jit(solution)/shard_map/reduce_scatter | solution.py:108
  81.4 4.5 %copy-start.2 = (bf16[64,512]{1,0:T(8,128)(2,1)}, bf16[64,512]{1,0:T(8,128)(2,1)S(1)}, u32[]{:S(2)}) copy-start(bf16[64,512]{1,0:T(8,128)(2,1)S(1)} %scatter_custom_fusion.2) | copy-start | bytes 196612
  99.4 11.5 %all-to-all-start.5 = ((bf16[4,32,512]{2,0,1:T(4,128)(2,1)}), bf16[4,32,512]{2,0,1:T(4,128)(2,1)S(1)}, u32[]{:S(2)}, u32[]{:S(2)}) async-start(bf16[4,32,512]{2,0,1:T(4,128)(2,1)} %copy.128), calls=%async_computation.5 | async-start | bytes 262144 | tf_op jit(solution)/shard_map/all_to_all | solution.py:102
  110.9 21.0 %all-to-all-start.4 = ((bf16[4,32,2048]{2,0,1:T(4,128)(2,1)}), bf16[4,32,2048]{2,0,1:T(4,128)(2,1)S(1)}, u32[]{:S(2)}, u32[]{:S(2)}) async-start(bf16[4,32,2048]{2,0,1:T(4,128)(2,1)} %copy.125), calls=%async_computation.4 | async-start | bytes 1048576 | tf_op jit(solution)/shard_map/all_to_all | solution.py:101
Sparse Core Ops, SparseCore 0:
  86.1 149.8 reduce-scatter.1
where the time goes:
time: 245 us
  waiting for transfers between devices  148 us (60%)
  blocking collectives  28.5 us (12%)
  local copies, waits for them, and re-layouts  20.2 us (8%)
  starting transfers between devices  18.9 us (8%)
  between operations  14.4 us (6%)
  matrix products  9.95 us (4%)
  other arithmetic  4.25 us (2%)
    reduce_scatter x1, waiting for transfers between devices, local(): lax.psum_scatter(jnp.einsum('td,tc->dc', hidden_in, grad_values, preferre...  102 us
    all_to_all x1, blocking collectives, local(): lax.all_to_all(pack_rows(queries), 'dp', split_axis=1, concat_axis=1, til...  18 us
    all_to_all x1, waiting for transfers between devices, local(): lax.all_to_all(unflatten(grad_q_rows), 'dp', split_axis=1, concat_axis=1,...  16.7 us
    all_to_all x1, waiting for transfers between devices, local(): lax.all_to_all(pack_rows(grad_attn), 'dp', split_axis=1, concat_axis=1, t...  14.1 us
    all_to_all x1, blocking collectives, local(): lax.all_to_all(pack_rows(values), 'dp', split_axis=1, concat_axis=1, tile...  10.5 us
    all_to_all x1, waiting for transfers between devices, local(): lax.all_to_all(unflatten(grad_v_rows), 'dp', split_axis=1, concat_axis=1,...  8.09 us
    all_to_all x1, starting transfers between devices, local(): lax.all_to_all(pack_rows(keys), 'dp', split_axis=1, concat_axis=1, tiled=...  7.3 us
    gather x4, local copies, waits for them, and re-layouts, pack_rows(): table[pick_rows]  6.82 us
  transfers between devices with their start and end apart: 6, of which 6 were waited for; matrix products, arithmetic and copies ran while one was open for 7% of the time, Pallas kernels for 0%

commit v1 on v0

v1 whole, which is shorter than its diff:
```python
import functools
import math

import jax
import jax.numpy as jnp
from jax import lax
from jax.experimental import pallas as pl
from jax.experimental.pallas import tpu as pltpu
from jax.sharding import PartitionSpec as P

HQ = 16
HK = 4
DH = 128
PER_KV = HQ // HK
ROWS = 8
HALO = 3
TEAM = 8
MESH = pl.DeviceIdType.MESH
F32 = jnp.float32
BF16 = jnp.bfloat16

Q_AT = 0
O_AT = PER_KV * ROWS
K_AT = 2 * PER_KV * ROWS
V_AT = K_AT + 2 * ROWS
IN_ROWS = V_AT + 2 * ROWS
BACK_ROWS = PER_KV * ROWS + 2 * ROWS


def dot(a, b, da, db):
    return lax.dot_general(a, b, (((da,), (db,)), ((), ())), preferred_element_type=F32)


def wait_bytes(ref, count, sem):
    view = ref.at[pl.ds(0, count)]
    pltpu.make_async_copy(view, view, sem).wait()


def kernel(
    n, width,
    hid_ref, q_ref, k_ref, v_ref, o_ref, rows_ref, docs_ref,
    dq_ref, dk_ref, dv_ref, dw_ref,
    q32, o32, k32, v32, stage, came, probs, acc_v, acc_k,
    back_v, home_v, back, home, hid_out, hid_in, gv, gv_in, part, term_out, term_in,
    sent, got,
):
    me = lax.axis_index("dp")
    tok = q_ref.shape[0]
    groups = n // HK
    teams = n // TEAM
    member = lax.rem(me, TEAM)
    team = lax.div(me, TEAM)
    group = lax.div(me, HK)
    scale = 1.0 / math.sqrt(DH)
    keys = n * 2 * ROWS
    chunk = 8
    q_rows = chunk * PER_KV * ROWS

    barrier = pltpu.get_barrier_semaphore()

    def greet(i, c):
        pl.semaphore_signal(
            barrier, inc=1, device_id=(lax.rem(me + i, n),), device_id_type=MESH
        )
        return c

    lax.fori_loop(1, n, greet, 0)

    q32[...] = q_ref[...].astype(F32)
    o32[...] = o_ref[...].astype(F32)
    k32[0:ROWS, :] = jnp.zeros((ROWS, k32.shape[1]), F32)
    v32[0:ROWS, :] = jnp.zeros((ROWS, v32.shape[1]), F32)
    k32[ROWS:, :] = k_ref[...].astype(F32)
    v32[ROWS:, :] = v_ref[...].astype(F32)
    lane = lax.broadcasted_iota(jnp.int32, (2 * ROWS, DH), 1)
    line = lax.broadcasted_iota(jnp.int32, (2 * ROWS, DH), 0)
    doc_line = jnp.zeros((2 * ROWS, DH), F32)
    for j in range(docs_ref.shape[1]):
        doc_line = jnp.where(lane == j, (docs_ref[0, j] + 1).astype(F32), doc_line)

    def pack(g, c):
        at = pl.multiple_of(g * ROWS, ROWS)
        for h in range(HK):
            parts = [
                table[pl.ds(at, ROWS), pl.ds((PER_KV * h + i) * DH, DH)]
                for table in (q32, o32)
                for i in range(PER_KV)
            ]
            k_part = k32[pl.ds(at, 2 * ROWS), pl.ds(h * DH, DH)]
            parts.append(jnp.where(line == 0, doc_line, k_part))
            parts.append(v32[pl.ds(at, 2 * ROWS), pl.ds(h * DH, DH)])
            stage[HK * g + h] = jnp.concatenate(parts, axis=0).astype(BF16)
        return c

    lax.fori_loop(0, groups, pack, 0)
    came[me] = stage[me]

    pl.semaphore_wait(barrier, n - 1)

    def to_all(src, dst, index):
        def send(i, c):
            peer = lax.rem(me + i, n)
            pltpu.make_async_remote_copy(
                src.at[peer], dst.at[me], sent.at[index], got.at[index],
                device_id=(peer,), device_id_type=MESH,
            ).start()
            return c

        lax.fori_loop(1, n, send, 0)

    def to_team(src_of, dst, index):
        for i in range(1, TEAM):
            other = lax.rem(member + i, TEAM)
            pltpu.make_async_remote_copy(
                src_of(other), dst.at[member], sent.at[index], got.at[index],
                device_id=(team * TEAM + other,), device_id_type=MESH,
            ).start()

    to_all(stage, came, 0)

    span = hid_out.shape[2]
    for m in range(TEAM):
        if width % DH == 0:
            for p in range(teams):
                hid_out[m, :, p * width : (p + 1) * width] = hid_ref[
                    :, (p * TEAM + m) * width : (p * TEAM + m + 1) * width
                ]
        else:
            hid_out[m] = hid_ref[:, m * span : (m + 1) * span]
    hid_in[member] = hid_out[member]
    to_team(lambda other: hid_out.at[other], hid_in, 1)

    acc_v[...] = jnp.zeros_like(acc_v)
    acc_k[...] = jnp.zeros_like(acc_k)
    home_v[n:, :, :] = jnp.zeros((HK, 2 * ROWS, DH), BF16)
    home[n:, :, :] = jnp.zeros((HK, BACK_ROWS, DH), BF16)

    wait_bytes(came, n - 1, got.at[0])

    doc_rows = came[:, K_AT : K_AT + 2 * ROWS, :].reshape(n, 2 * ROWS, DH)[:, 0, :]
    pick = (
        lax.broadcasted_iota(jnp.int32, (8, DH), 0) == lax.broadcasted_iota(jnp.int32, (8, DH), 1)
    ).astype(F32).astype(BF16)
    doc_table = dot(pick, doc_rows, 1, 1)
    loc = lax.broadcasted_iota(jnp.int32, (2 * ROWS, n), 0) + (group - 1) * ROWS
    doc_sum = jnp.zeros((2 * ROWS, n), F32)
    for j in range(rows_ref.shape[0]):
        doc_sum += jnp.where(rows_ref[j : j + 1, :] == loc, doc_table[j : j + 1, :], 0.0)
    docs = jnp.sum(doc_sum, axis=1, keepdims=True)
    own_docs = docs[ROWS:]
    back_count = jnp.zeros((ROWS, 1), F32)
    for d in range(1, HALO + 1):
        back_count += jnp.where(docs[ROWS - d : 2 * ROWS - d] == own_docs, 1.0, 0.0)
    first = (
        lax.broadcasted_iota(jnp.int32, (ROWS, 1), 0) - back_count.astype(jnp.int32)
    ) * n
    first = jnp.broadcast_to(first[None], (q_rows // ROWS, ROWS, 1)).reshape(q_rows, 1)
    col = lax.broadcasted_iota(jnp.int32, (1, keys), 1)
    k_pos = (lax.rem(col, 2 * ROWS) - ROWS) * n + lax.div(col, 2 * ROWS)
    row = lax.broadcasted_iota(jnp.int32, (q_rows, 1), 0)
    q_pos = lax.rem(row, ROWS) * n + lax.div(row, PER_KV * ROWS)

    def rows_of(c, at):
        return came[pl.ds(c * chunk, chunk), at : at + PER_KV * ROWS, :].reshape(q_rows, DH)

    def keys_of(at):
        return came[:, at : at + 2 * ROWS, :].reshape(keys, DH)

    def prob_of(c):
        scores = dot(rows_of(c, Q_AT), keys_of(K_AT), 1, 1) * scale
        allowed = (k_pos >= first) & (k_pos <= q_pos + c * chunk)
        scores = jnp.where(allowed, scores, -1000000000.0)
        weights = jnp.exp(scores - jnp.max(scores, axis=1, keepdims=True))
        return weights * (1.0 / jnp.sum(weights, axis=1, keepdims=True))

    def soft(c, carry):
        p = prob_of(c)
        if probs.shape[0] > q_rows:
            probs[pl.ds(pl.multiple_of(c * q_rows, q_rows), q_rows), :] = p
        acc_v[...] += dot(p.astype(BF16), rows_of(c, O_AT), 0, 0)
        return carry

    lax.fori_loop(0, n // chunk, soft, 0)
    back_v[...] = acc_v[...].reshape(n, 2 * ROWS, DH).astype(BF16)
    home_v[me] = back_v[me]
    to_all(back_v, home_v, 2)

    def grads(c, carry):
        if probs.shape[0] > q_rows:
            p = probs[pl.ds(pl.multiple_of(c * q_rows, q_rows), q_rows), :]
        else:
            p = prob_of(c)
        dprob = dot(rows_of(c, O_AT), keys_of(V_AT), 1, 1)
        delta = jnp.sum(p * dprob, axis=1, keepdims=True)
        dscore = (p * (dprob - delta) * scale).astype(BF16)
        dq = dot(dscore, keys_of(K_AT), 1, 0).astype(BF16)
        back[pl.ds(c * chunk, chunk), 0 : PER_KV * ROWS, :] = dq.reshape(chunk, PER_KV * ROWS, DH)
        acc_k[...] += dot(dscore, rows_of(c, Q_AT), 0, 0)
        return carry

    lax.fori_loop(0, n // chunk, grads, 0)
    back[:, PER_KV * ROWS :, :] = acc_k[...].reshape(n, 2 * ROWS, DH).astype(BF16)
    home[me] = back[me]
    to_all(back, home, 3)

    def summed(ref, g, h, at):
        own = ref[HK * g + h, at : at + 2 * ROWS, :].astype(F32)
        after = ref[HK * g + HK + h, at : at + 2 * ROWS, :].astype(F32)
        return own[ROWS:] + after[:ROWS]

    wait_bytes(home_v, n - 1, got.at[2])

    def place_v(pair, c):
        at = pl.multiple_of(pair * 2 * ROWS, 2 * ROWS)
        for h in range(HK):
            both = [summed(home_v, 2 * pair + s, h, 0) for s in range(2)]
            gv[pl.ds(at, 2 * ROWS), pl.ds(h * DH, DH)] = jnp.concatenate(both, axis=0).astype(BF16)
        return c

    lax.fori_loop(0, groups // 2, place_v, 0)
    to_team(lambda other: gv, gv_in, 4)
    gv_in[member] = gv[...]
    dv_ref[...] = gv[...]
    wait_bytes(hid_in, TEAM - 1, got.at[1])
    wait_bytes(gv_in, TEAM - 1, got.at[4])

    grad_scale = 1.0 / math.sqrt(tok * n)
    all_gv = gv_in[...].reshape(TEAM * tok, gv.shape[1])
    for c in range(span // DH):
        h_cols = hid_in[:, :, c * DH : (c + 1) * DH].reshape(TEAM * tok, DH)
        part[c * DH : (c + 1) * DH, :] = dot(h_cols, all_gv, 0, 0) * grad_scale
    term_out[...] = part[...].reshape(teams, width, part.shape[1]).astype(BF16)
    for i in range(1, teams):
        other = lax.rem(team + i, teams)
        pltpu.make_async_remote_copy(
            term_out.at[other], term_in.at[team], sent.at[5], got.at[5],
            device_id=(other * TEAM + member,), device_id_type=MESH,
        ).start()

    wait_bytes(home, n - 1, got.at[3])

    def place(pair, c):
        at = pl.multiple_of(pair * 2 * ROWS, 2 * ROWS)
        for h in range(HK):
            both = [summed(home, 2 * pair + s, h, PER_KV * ROWS) for s in range(2)]
            dk_ref[pl.ds(at, 2 * ROWS), pl.ds(h * DH, DH)] = jnp.concatenate(
                both, axis=0
            ).astype(BF16)
            lower = home[HK * 2 * pair + h, 0 : PER_KV * ROWS, :].astype(F32)
            upper = home[HK * (2 * pair + 1) + h, 0 : PER_KV * ROWS, :].astype(F32)
            for i in range(PER_KV):
                cut = slice(i * ROWS, (i + 1) * ROWS)
                dq_ref[pl.ds(at, 2 * ROWS), pl.ds((PER_KV * h + i) * DH, DH)] = jnp.concatenate(
                    [lower[cut], upper[cut]], axis=0
                ).astype(BF16)
        return c

    lax.fori_loop(0, groups // 2, place, 0)

    wait_bytes(term_in, teams - 1, got.at[5])
    total = part[pl.ds(pl.multiple_of(team * width, width), width), :]
    for i in range(1, teams):
        total += term_in[lax.rem(team + i, teams)].astype(F32)
    dw_ref[...] = total

    wait_bytes(stage, n - 1, sent.at[0])
    wait_bytes(hid_out, TEAM - 1, sent.at[1])
    wait_bytes(back_v, n - 1, sent.at[2])
    wait_bytes(back, n - 1, sent.at[3])
    wait_bytes(gv_in, TEAM - 1, sent.at[4])
    wait_bytes(term_out, teams - 1, sent.at[5])


def local(hidden_in, queries, keys, values, grad_attn, send_rows, slot_docs):
    n = lax.axis_size("dp")
    tok, model = hidden_in.shape
    width = model // n
    teams = n // TEAM
    span = model // TEAM
    kv = keys.shape[1]
    if width % DH:
        hidden_in = (
            hidden_in.reshape(tok, teams, TEAM, width).swapaxes(1, 2).reshape(tok, model)
        )
    vmem = pl.BlockSpec(memory_space=pltpu.VMEM)
    smem = pl.BlockSpec(memory_space=pltpu.SMEM)
    owned = 2 * ROWS
    return pl.pallas_call(
        functools.partial(kernel, n, width),
        out_shape=(
            jax.ShapeDtypeStruct(queries.shape, BF16),
            jax.ShapeDtypeStruct(keys.shape, BF16),
            jax.ShapeDtypeStruct(values.shape, BF16),
            jax.ShapeDtypeStruct((width, kv), F32),
        ),
        in_specs=[vmem] * 6 + [smem],
        out_specs=(vmem,) * 4,
        scratch_shapes=[
            pltpu.VMEM(queries.shape, F32),
            pltpu.VMEM(queries.shape, F32),
            pltpu.VMEM((tok + ROWS, kv), F32),
            pltpu.VMEM((tok + ROWS, kv), F32),
            pltpu.VMEM((n, IN_ROWS, DH), BF16),
            pltpu.VMEM((n, IN_ROWS, DH), BF16),
            pltpu.VMEM((n * PER_KV * ROWS if n <= 64 else ROWS, n * owned), F32),
            pltpu.VMEM((n * owned, DH), F32),
            pltpu.VMEM((n * owned, DH), F32),
            pltpu.VMEM((n, owned, DH), BF16),
            pltpu.VMEM((n + HK, owned, DH), BF16),
            pltpu.VMEM((n, BACK_ROWS, DH), BF16),
            pltpu.VMEM((n + HK, BACK_ROWS, DH), BF16),
            pltpu.VMEM((TEAM, tok, span), BF16),
            pltpu.VMEM((TEAM, tok, span), BF16),
            pltpu.VMEM((tok, kv), BF16),
            pltpu.VMEM((TEAM, tok, kv), BF16),
            pltpu.VMEM((span, kv), F32),
            pltpu.VMEM((teams, width, kv), BF16),
            pltpu.VMEM((teams, width, kv), BF16),
            pltpu.SemaphoreType.DMA((6,)),
            pltpu.SemaphoreType.DMA((6,)),
        ],
        compiler_params=pltpu.CompilerParams(
            collective_id=0,
            has_side_effects=True,
            vmem_limit_bytes=(60 if n > 64 else 40) * 2**20,
        ),
    )(hidden_in, queries, keys, values, grad_attn, send_rows, slot_docs)


def solution(mesh):
    placed = (
        P("dp", None),
        P("dp", None),
        P("dp", None),
        P("dp", None),
        P("dp", None),
        P(),
        P("dp", None),
    )
    return jax.shard_map(
        local,
        mesh=mesh,
        in_specs=placed,
        out_specs=(P("dp", None), P("dp", None), P("dp", None), P("dp", None)),
        check_vma=False,
    )
```

time: 245 us -> 65.9 us (0.27)
  waiting for transfers between devices: 148 us -> 0 us
  Pallas kernels: 0 us -> 55.6 us
  blocking collectives: 28.5 us -> 0 us
  starting transfers between devices: 18.9 us -> 0 us
  between operations: 14.4 us -> 0.66 us
  local copies, waits for them, and re-layouts: 20.2 us -> 8.61 us
  matrix products: 9.95 us -> 0 us
  other arithmetic: 4.25 us -> 0 us
    reduce_scatter x1 -> x0, waiting for transfers between devices: 102 us -> none  [local(): lax.psum_scatter(jnp.einsum('td,tc->dc', hidden_in, grad_values, preferre...]
    pallas_call x0 -> x1, Pallas kernels: none -> 55.6 us  [local(): pl.pallas_call(functools.partial(kernel, n, width), out_shape=(jax.ShapeD...]
    all_to_all x5 -> x0, waiting for transfers between devices: 46.7 us -> none  [the longest x1 16.7 us: local(): lax.all_to_all(unflatten(grad_q_rows), 'dp', split_axis=1, concat_axis=1,...]
    all_to_all x2 -> x0, blocking collectives: 28.5 us -> none  [the longest x1 18 us: local(): lax.all_to_all(pack_rows(queries), 'dp', split_axis=1, concat_axis=1, til...]
    all_to_all x5 -> x0, starting transfers between devices: 18.8 us -> none  [the longest x1 7.3 us: local(): lax.all_to_all(pack_rows(keys), 'dp', split_axis=1, concat_axis=1, tiled=...]
    dot_general x17 -> x0, matrix products: 8.9 us -> none  [the longest x1 4.49 us: local(): jnp.einsum('td,tc->dc', hidden_in, grad_values, preferred_element_type=jn...]
    gather x4 -> x0, local copies, waits for them, and re-layouts: 6.82 us -> none  [pack_rows(): table[pick_rows]]
    unnamed x11 -> x18, local copies, waits for them, and re-layouts: 1.81 us -> 8.61 us
  transfers between devices with their start and end apart: 6 -> 0, of which waited for: 6 -> 0; matrix products, arithmetic and copies ran while one was open for 7% -> 0% of each run, Pallas kernels for 0% -> 0%
where the time goes in v1:
time: 65.9 us; the launch traced here: 64.9 us
  Pallas kernels  55.6 us (84%)
  local copies, waits for them, and re-layouts  8.61 us (13%)
  between operations  0.66 us (1%)
    pallas_call x1, Pallas kernels, local(): pl.pallas_call(functools.partial(kernel, n, width), out_shape=(jax.ShapeD...  55.6 us
    unnamed x18, local copies, waits for them, and re-layouts  8.61 us

profile of v1, /device:TPU:0, one launch (start us, length us, event | category | flops | bytes accessed | tf_op | source)
XLA Modules:
  0.0 64.9 jit_solution(3525784277535344682)
XLA Ops:
  0.6 0.0 copy-start
  0.6 1.0 %copy-done = bf16[64,4096]{1,0:T(8,128)(2,1)S(1)} copy-done((bf16[64,4096]{1,0:T(8,128)(2,1)S(1)}, bf16[64,4096]{1,0:T(8,128)(2,1)}, u32[]{:S(2)}) %copy-start) | copy-done | bytes 524312
  1.7 0.0 copy-start.1
  1.7 0.9 %copy-done.1 = bf16[64,2048]{1,0:T(8,128)(2,1)S(1)} copy-done((bf16[64,2048]{1,0:T(8,128)(2,1)S(1)}, bf16[64,2048]{1,0:T(8,128)(2,1)}, u32[]{:S(2)}) %copy-start.1) | copy-done | bytes 262168
  2.6 0.0 copy-start.2
  2.6 0.9 %copy-done.2 = bf16[64,2048]{1,0:T(8,128)(2,1)S(1)} copy-done((bf16[64,2048]{1,0:T(8,128)(2,1)S(1)}, bf16[64,2048]{1,0:T(8,128)(2,1)}, u32[]{:S(2)}) %copy-start.2) | copy-done | bytes 262168
  3.6 0.0 copy-start.3
  3.6 0.8 %copy-done.3 = bf16[64,512]{1,0:T(8,128)(2,1)S(1)} copy-done((bf16[64,512]{1,0:T(8,128)(2,1)S(1)}, bf16[64,512]{1,0:T(8,128)(2,1)}, u32[]{:S(2)}) %copy-start.3) | copy-done | bytes 65560
  4.4 0.0 copy-start.4
  4.4 0.8 %copy-done.4 = bf16[64,512]{1,0:T(8,128)(2,1)S(1)} copy-done((bf16[64,512]{1,0:T(8,128)(2,1)S(1)}, bf16[64,512]{1,0:T(8,128)(2,1)}, u32[]{:S(2)}) %copy-start.4) | copy-done | bytes 65560
  5.3 0.0 copy-start.5
  5.3 0.7 %copy-done.5 = s32[4,32]{1,0:T(4,128)S(1)} copy-done((s32[4,32]{1,0:T(4,128)S(1)}, s32[4,32]{1,0:T(4,128)}, u32[]{:S(2)}) %copy-start.5) | copy-done | bytes 536
  5.9 0.0 copy-start.6
  5.9 0.7 %copy-done.6 = s32[1,4]{1,0:T(1,128)S(1)} copy-done((s32[1,4]{1,0:T(1,128)S(1)}, s32[1,4]{1,0:T(1,128)}, u32[]{:S(2)}) %copy-start.6) | copy-done | bytes 40
  6.6 55.6 %shard_map.102 = (bf16[64,2048]{1,0:T(8,128)(2,1)S(1)}, bf16[64,512]{1,0:T(8,128)(2,1)S(1)}, bf16[64,512]{1,0:T(8,128)(2,1)S(1)}, f32[128,512]{1,0:T(8,128)S(1)}) custom-call(bf16[64,4096]{1,0:T(8,128)(2,1)S(1)} %copy-done, bf16[64,2048]{1,0:T(8,128)(2,1)S(1)} %copy-done.1, bf16[64,512]{1,0:T(8,128)(2,1)S(1)} %copy-done.3, bf16[64,512]{1,0:T(8,128)(2,1)S(1)} %copy-done.4, ...), custom_call_target="tpu_custom_call" | custom-call | tf_op jit(solution)/shard_map/pallas_call | solution.py:288
  62.2 0.7 %copy.15 = bf16[64,2048]{1,0:T(8,128)(2,1)} copy(bf16[64,2048]{1,0:T(8,128)(2,1)S(1)} %get-tuple-element.8) | data formatting | bytes 524288
  62.9 0.6 copy.16
  63.5 0.6 copy.17
  64.2 0.7 %copy.18 = f32[128,512]{1,0:T(8,128)} copy(f32[128,512]{1,0:T(8,128)S(1)} %get-tuple-element.11) | data formatting | bytes 524288
Async XLA Ops:
  0.6 1.0 %copy-start = (bf16[64,4096]{1,0:T(8,128)(2,1)S(1)}, bf16[64,4096]{1,0:T(8,128)(2,1)}, u32[]{:S(2)}) copy-start(bf16[64,4096]{1,0:T(8,128)(2,1)} %hid_ref.1) | copy-start | bytes 1572868
  1.7 0.9 %copy-start.1 = (bf16[64,2048]{1,0:T(8,128)(2,1)S(1)}, bf16[64,2048]{1,0:T(8,128)(2,1)}, u32[]{:S(2)}) copy-start(bf16[64,2048]{1,0:T(8,128)(2,1)} %q_ref.1) | copy-start | bytes 786436
  2.6 0.9 %copy-start.2 = (bf16[64,2048]{1,0:T(8,128)(2,1)S(1)}, bf16[64,2048]{1,0:T(8,128)(2,1)}, u32[]{:S(2)}) copy-start(bf16[64,2048]{1,0:T(8,128)(2,1)} %o_ref.1) | copy-start | bytes 786436
  3.6 0.8 %copy-start.3 = (bf16[64,512]{1,0:T(8,128)(2,1)S(1)}, bf16[64,512]{1,0:T(8,128)(2,1)}, u32[]{:S(2)}) copy-start(bf16[64,512]{1,0:T(8,128)(2,1)} %k_ref.1) | copy-start | bytes 196612
  4.4 0.8 %copy-start.4 = (bf16[64,512]{1,0:T(8,128)(2,1)S(1)}, bf16[64,512]{1,0:T(8,128)(2,1)}, u32[]{:S(2)}) copy-start(bf16[64,512]{1,0:T(8,128)(2,1)} %v_ref.1) | copy-start | bytes 196612
  5.3 0.7 %copy-start.5 = (s32[4,32]{1,0:T(4,128)S(1)}, s32[4,32]{1,0:T(4,128)}, u32[]{:S(2)}) copy-start(s32[4,32]{1,0:T(4,128)} %rows_ref.1) | copy-start | bytes 1540
  5.9 0.7 %copy-start.6 = (s32[1,4]{1,0:T(1,128)S(1)}, s32[1,4]{1,0:T(1,128)}, u32[]{:S(2)}) copy-start(s32[1,4]{1,0:T(1,128)} %docs_ref.1) | copy-start | bytes 52

commit v2 on v1

v2 whole, which is shorter than its diff:
```python
import functools
import math

import jax
import jax.numpy as jnp
from jax import lax
from jax.experimental import pallas as pl
from jax.experimental.pallas import tpu as pltpu
from jax.sharding import PartitionSpec as P

HQ = 16
HK = 4
DH = 128
PER_KV = HQ // HK
ROWS = 8
HALO = 3
TEAM = 8
MESH = pl.DeviceIdType.MESH
F32 = jnp.float32
BF16 = jnp.bfloat16

HEAD_ROWS = PER_KV * ROWS
MSG_ROWS = HEAD_ROWS + 2 * ROWS


def dot(a, b, da, db):
    return lax.dot_general(a, b, (((da,), (db,)), ((), ())), preferred_element_type=F32)


def wait_bytes(ref, count, sem):
    view = ref.at[pl.ds(0, count)]
    pltpu.make_async_copy(view, view, sem).wait()


def kernel(
    n, width,
    hid_hbm, q_hbm, k_hbm, v_hbm, o_hbm, rows_hbm, docs_hbm,
    dq_hbm, dk_hbm, dv_hbm, dw_hbm,
    hid_ref, q_ref, k_ref, v_ref, o_ref, rows_ref, docs_ref, dq_ref, dk_ref, dw_ref,
    q32, o32, k32, v32, stage_s, came_s, stage_g, came_g, probs, acc_v, acc_k,
    back_v, home_v, back, home, hid_out, hid_in, hid_t, gv, gv_in, term_out, term_in,
    loaded, stored, sent, got,
):
    me = lax.axis_index("dp")
    tok = q_ref.shape[0]
    groups = n // HK
    teams = n // TEAM
    member = lax.rem(me, TEAM)
    team = lax.div(me, TEAM)
    group = lax.div(me, HK)
    scale = 1.0 / math.sqrt(DH)
    keys = n * 2 * ROWS
    chunk = 8
    q_rows = chunk * PER_KV * ROWS

    loads = [
        pltpu.make_async_copy(src, dst, loaded.at[i])
        for i, (src, dst) in enumerate(
            (
                (q_hbm, q_ref),
                (k_hbm, k_ref),
                (docs_hbm, docs_ref),
                (o_hbm, o_ref),
                (v_hbm, v_ref),
                (hid_hbm, hid_ref),
                (rows_hbm, rows_ref),
            )
        )
    ]
    for load in loads:
        load.start()

    barrier = pltpu.get_barrier_semaphore()

    def greet(i, c):
        pl.semaphore_signal(
            barrier, inc=1, device_id=(lax.rem(me + i, n),), device_id_type=MESH
        )
        return c

    lax.fori_loop(1, n, greet, 0)

    k32[0:ROWS, :] = jnp.zeros((ROWS, k32.shape[1]), F32)
    v32[0:ROWS, :] = jnp.zeros((ROWS, v32.shape[1]), F32)
    for load in loads[:3]:
        load.wait()
    q32[...] = q_ref[...].astype(F32)
    k32[ROWS:, :] = k_ref[...].astype(F32)
    lane = lax.broadcasted_iota(jnp.int32, (2 * ROWS, DH), 1)
    line = lax.broadcasted_iota(jnp.int32, (2 * ROWS, DH), 0)
    doc_line = jnp.zeros((2 * ROWS, DH), F32)
    for j in range(docs_ref.shape[1]):
        doc_line = jnp.where(lane == j, (docs_ref[0, j] + 1).astype(F32), doc_line)

    def packer(dst, heads, tail, with_docs):
        def pack(g, c):
            at = pl.multiple_of(g * ROWS, ROWS)
            for h in range(HK):
                parts = [
                    heads[pl.ds(at, ROWS), pl.ds((PER_KV * h + i) * DH, DH)]
                    for i in range(PER_KV)
                ]
                part = tail[pl.ds(at, 2 * ROWS), pl.ds(h * DH, DH)]
                parts.append(jnp.where(line == 0, doc_line, part) if with_docs else part)
                dst[HK * g + h] = jnp.concatenate(parts, axis=0).astype(BF16)
            return c

        return pack

    def to_all(src, dst, index):
        def send(i, c):
            peer = lax.rem(me + i * (TEAM + 1), n)
            pltpu.make_async_remote_copy(
                src.at[peer], dst.at[me], sent.at[index], got.at[index],
                device_id=(peer,), device_id_type=MESH,
            ).start()
            return c

        lax.fori_loop(1, n, send, 0)

    def to_team(src_of, dst, index):
        for i in range(1, TEAM):
            other = lax.rem(member + i, TEAM)
            pltpu.make_async_remote_copy(
                src_of(other), dst.at[member], sent.at[index], got.at[index],
                device_id=(team * TEAM + other,), device_id_type=MESH,
            ).start()

    lax.fori_loop(0, groups, packer(stage_s, q32, k32, True), 0)
    pl.semaphore_wait(barrier, n - 1)
    to_all(stage_s, came_s, 0)

    for load in loads[3:5]:
        load.wait()
    o32[...] = o_ref[...].astype(F32)
    v32[ROWS:, :] = v_ref[...].astype(F32)
    lax.fori_loop(0, groups, packer(stage_g, o32, v32, False), 0)
    to_all(stage_g, came_g, 6)

    for load in loads[5:]:
        load.wait()
    span = hid_out.shape[2]
    for m in range(TEAM):
        if width % DH == 0:
            for p in range(teams):
                hid_out[m, :, p * width : (p + 1) * width] = hid_ref[
                    :, (p * TEAM + m) * width : (p * TEAM + m + 1) * width
                ]
        else:
            hid_out[m] = hid_ref[:, m * span : (m + 1) * span]
    to_team(lambda other: hid_out.at[other], hid_in, 1)
    hid_in[member] = hid_out[member]

    came_s[me] = stage_s[me]
    came_g[me] = stage_g[me]
    acc_v[...] = jnp.zeros_like(acc_v)
    acc_k[...] = jnp.zeros_like(acc_k)
    home_v[n:, :, :] = jnp.zeros((HK, 2 * ROWS, DH), BF16)
    home[n:, :, :] = jnp.zeros((HK, MSG_ROWS, DH), BF16)

    wait_bytes(came_s, n - 1, got.at[0])

    doc_rows = came_s[:, HEAD_ROWS:, :][:, 0, :]
    pick = (
        lax.broadcasted_iota(jnp.int32, (8, DH), 0) == lax.broadcasted_iota(jnp.int32, (8, DH), 1)
    ).astype(F32).astype(BF16)
    doc_table = dot(pick, doc_rows, 1, 1)
    loc = lax.broadcasted_iota(jnp.int32, (2 * ROWS, n), 0) + (group - 1) * ROWS
    doc_sum = jnp.zeros((2 * ROWS, n), F32)
    for j in range(rows_ref.shape[0]):
        doc_sum += jnp.where(rows_ref[j : j + 1, :] == loc, doc_table[j : j + 1, :], 0.0)
    docs = jnp.sum(doc_sum, axis=1, keepdims=True)
    own_docs = docs[ROWS:]
    back_count = jnp.zeros((ROWS, 1), F32)
    for d in range(1, HALO + 1):
        back_count += jnp.where(docs[ROWS - d : 2 * ROWS - d] == own_docs, 1.0, 0.0)
    first = (
        lax.broadcasted_iota(jnp.int32, (ROWS, 1), 0) - back_count.astype(jnp.int32)
    ) * n
    first = jnp.broadcast_to(first[None], (q_rows // ROWS, ROWS, 1)).reshape(q_rows, 1)
    col = lax.broadcasted_iota(jnp.int32, (1, keys), 1)
    k_pos = (lax.rem(col, 2 * ROWS) - ROWS) * n + lax.div(col, 2 * ROWS)
    row = lax.broadcasted_iota(jnp.int32, (q_rows, 1), 0)
    q_pos = lax.rem(row, ROWS) * n + lax.div(row, HEAD_ROWS)

    def rows_of(ref, c):
        return ref[pl.ds(c * chunk, chunk), 0:HEAD_ROWS, :].reshape(q_rows, DH)

    def keys_of(ref):
        return ref[:, HEAD_ROWS:, :].reshape(keys, DH)

    def prob_of(c):
        scores = dot(rows_of(came_s, c), keys_of(came_s), 1, 1) * scale
        allowed = (k_pos >= first) & (k_pos <= q_pos + c * chunk)
        scores = jnp.where(allowed, scores, -1000000000.0)
        weights = jnp.exp(scores - jnp.max(scores, axis=1, keepdims=True))
        return weights * (1.0 / jnp.sum(weights, axis=1, keepdims=True))

    kept = probs.shape[0] > q_rows

    def prob_rows(c):
        return pl.ds(pl.multiple_of(c * q_rows, q_rows), q_rows)

    def soft(c, carry):
        probs[prob_rows(c), :] = prob_of(c)
        return carry

    if kept:
        lax.fori_loop(0, n // chunk, soft, 0)

    wait_bytes(came_g, n - 1, got.at[6])

    def value_grads(c, carry):
        p = probs[prob_rows(c), :] if kept else prob_of(c)
        acc_v[...] += dot(p.astype(BF16), rows_of(came_g, c), 0, 0)
        return carry

    lax.fori_loop(0, n // chunk, value_grads, 0)
    back_v[...] = acc_v[...].reshape(n, 2 * ROWS, DH).astype(BF16)
    to_all(back_v, home_v, 2)
    home_v[me] = back_v[me]

    def grads(c, carry):
        p = probs[prob_rows(c), :] if kept else prob_of(c)
        dprob = dot(rows_of(came_g, c), keys_of(came_g), 1, 1)
        delta = jnp.sum(p * dprob, axis=1, keepdims=True)
        dscore = (p * (dprob - delta) * scale).astype(BF16)
        dq = dot(dscore, keys_of(came_s), 1, 0).astype(BF16)
        back[pl.ds(c * chunk, chunk), 0:HEAD_ROWS, :] = dq.reshape(chunk, HEAD_ROWS, DH)
        acc_k[...] += dot(dscore, rows_of(came_s, c), 0, 0)
        return carry

    lax.fori_loop(0, n // chunk, grads, 0)
    back[:, HEAD_ROWS:, :] = acc_k[...].reshape(n, 2 * ROWS, DH).astype(BF16)
    to_all(back, home, 3)
    home[me] = back[me]

    wait_bytes(hid_in, TEAM - 1, got.at[1])
    tile = DH // min(tok, DH)
    for t in range(TEAM * tok // DH):
        if tile > 1:
            rows = hid_in[t * tile : (t + 1) * tile].reshape(DH, span)
        else:
            per = tok // DH
            rows = hid_in[t // per, (t % per) * DH : (t % per + 1) * DH, :]
        hid_t[:, t * DH : (t + 1) * DH] = rows.T

    def summed(ref, g, h, at):
        own = ref[HK * g + h, at : at + 2 * ROWS, :].astype(F32)
        after = ref[HK * g + HK + h, at : at + 2 * ROWS, :].astype(F32)
        return own[ROWS:] + after[:ROWS]

    wait_bytes(home_v, n - 1, got.at[2])

    def place_v(pair, c):
        at = pl.multiple_of(pair * 2 * ROWS, 2 * ROWS)
        for h in range(HK):
            both = [summed(home_v, 2 * pair + s, h, 0) for s in range(2)]
            gv[pl.ds(at, 2 * ROWS), pl.ds(h * DH, DH)] = jnp.concatenate(both, axis=0).astype(BF16)
        return c

    lax.fori_loop(0, groups // 2, place_v, 0)
    to_team(lambda other: gv, gv_in, 4)
    store_v = pltpu.make_async_copy(gv, dv_hbm, stored.at[0])
    store_v.start()
    gv_in[member] = gv[...]
    wait_bytes(gv_in, TEAM - 1, got.at[4])

    grad_scale = 1.0 / math.sqrt(tok * n)

    def term(p):
        cols = hid_t[pl.ds(pl.multiple_of(p * width, width), width), :]
        return dot(cols, gv_in[...].reshape(TEAM * tok, gv.shape[1]), 1, 0) * grad_scale

    for i in range(1, teams):
        other = lax.rem(team + i, teams)
        term_out[other] = term(other).astype(BF16)
        pltpu.make_async_remote_copy(
            term_out.at[other], term_in.at[team], sent.at[5], got.at[5],
            device_id=(other * TEAM + member,), device_id_type=MESH,
        ).start()
    dw_ref[...] = term(team)

    wait_bytes(home, n - 1, got.at[3])

    def place(pair, c):
        at = pl.multiple_of(pair * 2 * ROWS, 2 * ROWS)
        for h in range(HK):
            both = [summed(home, 2 * pair + s, h, HEAD_ROWS) for s in range(2)]
            dk_ref[pl.ds(at, 2 * ROWS), pl.ds(h * DH, DH)] = jnp.concatenate(
                both, axis=0
            ).astype(BF16)
            lower = home[HK * 2 * pair + h, 0:HEAD_ROWS, :].astype(F32)
            upper = home[HK * (2 * pair + 1) + h, 0:HEAD_ROWS, :].astype(F32)
            for i in range(PER_KV):
                cut = slice(i * ROWS, (i + 1) * ROWS)
                dq_ref[pl.ds(at, 2 * ROWS), pl.ds((PER_KV * h + i) * DH, DH)] = jnp.concatenate(
                    [lower[cut], upper[cut]], axis=0
                ).astype(BF16)
        return c

    lax.fori_loop(0, groups // 2, place, 0)
    store_q = pltpu.make_async_copy(dq_ref, dq_hbm, stored.at[1])
    store_k = pltpu.make_async_copy(dk_ref, dk_hbm, stored.at[2])
    store_q.start()
    store_k.start()

    wait_bytes(term_in, teams - 1, got.at[5])
    total = dw_ref[...]
    for i in range(1, teams):
        total += term_in[lax.rem(team + i, teams)].astype(F32)
    dw_ref[...] = total
    store_w = pltpu.make_async_copy(dw_ref, dw_hbm, stored.at[3])
    store_w.start()

    wait_bytes(stage_s, n - 1, sent.at[0])
    wait_bytes(stage_g, n - 1, sent.at[6])
    wait_bytes(hid_out, TEAM - 1, sent.at[1])
    wait_bytes(back_v, n - 1, sent.at[2])
    wait_bytes(back, n - 1, sent.at[3])
    wait_bytes(gv_in, TEAM - 1, sent.at[4])
    wait_bytes(term_out, teams - 1, sent.at[5])
    store_v.wait()
    store_q.wait()
    store_k.wait()
    store_w.wait()


def hand_over(*refs):
    count = (len(refs) - 2) // 3
    srcs, dsts, held = refs[:count], refs[count : 2 * count], refs[2 * count : 3 * count]
    in_sem, out_sem = refs[3 * count :]
    ins = [pltpu.make_async_copy(srcs[i], held[i], in_sem.at[i]) for i in range(count)]
    outs = [pltpu.make_async_copy(held[i], dsts[i], out_sem.at[i]) for i in range(count)]
    for copy in ins:
        copy.start()
    for i in range(count):
        ins[i].wait()
        outs[i].start()
    for copy in outs:
        copy.wait()


def local(hidden_in, queries, keys, values, grad_attn, send_rows, slot_docs):
    n = lax.axis_size("dp")
    tok, model = hidden_in.shape
    width = model // n
    teams = n // TEAM
    span = model // TEAM
    kv = keys.shape[1]
    if width % DH:
        hidden_in = (
            hidden_in.reshape(tok, teams, TEAM, width).swapaxes(1, 2).reshape(tok, model)
        )
    whole = pl.BlockSpec(memory_space=pl.ANY)
    owned = 2 * ROWS
    results = (
        jax.ShapeDtypeStruct(queries.shape, BF16),
        jax.ShapeDtypeStruct(keys.shape, BF16),
        jax.ShapeDtypeStruct(values.shape, BF16),
        jax.ShapeDtypeStruct((width, kv), F32),
    )
    outs = pl.pallas_call(
        functools.partial(kernel, n, width),
        out_shape=results,
        in_specs=[whole] * 7,
        out_specs=(whole,) * 4,
        scratch_shapes=[
            pltpu.VMEM(hidden_in.shape, BF16),
            pltpu.VMEM(queries.shape, BF16),
            pltpu.VMEM(keys.shape, BF16),
            pltpu.VMEM(values.shape, BF16),
            pltpu.VMEM(grad_attn.shape, BF16),
            pltpu.VMEM(send_rows.shape, jnp.int32),
            pltpu.SMEM(slot_docs.shape, jnp.int32),
            pltpu.VMEM(queries.shape, BF16),
            pltpu.VMEM(keys.shape, BF16),
            pltpu.VMEM((width, kv), F32),
            pltpu.VMEM(queries.shape, F32),
            pltpu.VMEM(queries.shape, F32),
            pltpu.VMEM((tok + ROWS, kv), F32),
            pltpu.VMEM((tok + ROWS, kv), F32),
            pltpu.VMEM((n, MSG_ROWS, DH), BF16),
            pltpu.VMEM((n, MSG_ROWS, DH), BF16),
            pltpu.VMEM((n, MSG_ROWS, DH), BF16),
            pltpu.VMEM((n, MSG_ROWS, DH), BF16),
            pltpu.VMEM((n * HEAD_ROWS if n <= 64 else ROWS, n * owned), F32),
            pltpu.VMEM((n * owned, DH), F32),
            pltpu.VMEM((n * owned, DH), F32),
            pltpu.VMEM((n, owned, DH), BF16),
            pltpu.VMEM((n + HK, owned, DH), BF16),
            pltpu.VMEM((n, MSG_ROWS, DH), BF16),
            pltpu.VMEM((n + HK, MSG_ROWS, DH), BF16),
            pltpu.VMEM((TEAM, tok, span), BF16),
            pltpu.VMEM((TEAM, tok, span), BF16),
            pltpu.VMEM((span, TEAM * tok), BF16),
            pltpu.VMEM((tok, kv), BF16),
            pltpu.VMEM((TEAM, tok, kv), BF16),
            pltpu.VMEM((teams, width, kv), BF16),
            pltpu.VMEM((teams, width, kv), BF16),
            pltpu.SemaphoreType.DMA((7,)),
            pltpu.SemaphoreType.DMA((4,)),
            pltpu.SemaphoreType.DMA((7,)),
            pltpu.SemaphoreType.DMA((7,)),
        ],
        compiler_params=pltpu.CompilerParams(
            collective_id=0, has_side_effects=True, vmem_limit_bytes=62 * 2**20
        ),
    )(hidden_in, queries, keys, values, grad_attn, send_rows, slot_docs)
    return pl.pallas_call(
        hand_over,
        out_shape=results,
        in_specs=[whole] * 4,
        out_specs=(whole,) * 4,
        scratch_shapes=[
            *(pltpu.VMEM(out.shape, out.dtype) for out in results),
            pltpu.SemaphoreType.DMA((4,)),
            pltpu.SemaphoreType.DMA((4,)),
        ],
        compiler_params=pltpu.CompilerParams(vmem_limit_bytes=62 * 2**20),
    )(*outs)


def solution(mesh):
    placed = (
        P("dp", None),
        P("dp", None),
        P("dp", None),
        P("dp", None),
        P("dp", None),
        P(),
        P("dp", None),
    )
    return jax.shard_map(
        local,
        mesh=mesh,
        in_specs=placed,
        out_specs=(P("dp", None), P("dp", None), P("dp", None), P("dp", None)),
        check_vma=False,
    )
```

time: 65.9 us -> 56.8 us (0.86)
  local copies, waits for them, and re-layouts: 8.61 us -> 0 us
    unnamed x18 -> x0, local copies, waits for them, and re-layouts: 8.61 us -> none
    pallas_call x1 -> x2, Pallas kernels: 55.6 us -> 55.4 us  [the longest x1 53.5 us: local(): pl.pallas_call(functools.partial(kernel, n, width), out_shape=results, in...]
where the time goes in v2:
time: 56.8 us; the launch traced here: 56 us
  Pallas kernels  55.4 us (98%)
  between operations  0.64 us (1%)
    pallas_call x1, Pallas kernels, local(): pl.pallas_call(functools.partial(kernel, n, width), out_shape=results, in...  53.5 us
    pallas_call x1, Pallas kernels, local(): pl.pallas_call(hand_over, out_shape=results, in_specs=[whole] * 4, out_sp...  1.86 us

profile of v2, /device:TPU:0, one launch (start us, length us, event | category | flops | bytes accessed | tf_op | source)
XLA Modules:
  0.0 56.0 jit_solution(16566983801013112811)
XLA Ops:
  0.6 53.5 %shard_map.102 = (bf16[64,2048]{1,0:T(8,128)(2,1)}, bf16[64,512]{1,0:T(8,128)(2,1)}, bf16[64,512]{1,0:T(8,128)(2,1)}, f32[128,512]{1,0:T(8,128)}) custom-call(bf16[64,4096]{1,0:T(8,128)(2,1)} %hid_hbm.1, bf16[64,2048]{1,0:T(8,128)(2,1)} %q_hbm.1, bf16[64,512]{1,0:T(8,128)(2,1)} %k_hbm.1, bf16[64,512]{1,0:T(8,128)(2,1)} %v_hbm.1, bf16[64,2048]{1,0:T(8,128)(2,1)} %o_hbm.1, ...), custom_call_target="tpu_custom_call" | custom-call | tf_op jit(solution)/shard_map/pallas_call | solution.py:363
  54.2 1.9 %shard_map.103 = (bf16[64,2048]{1,0:T(8,128)(2,1)}, bf16[64,512]{1,0:T(8,128)(2,1)}, bf16[64,512]{1,0:T(8,128)(2,1)}, f32[128,512]{1,0:T(8,128)}) custom-call(bf16[64,2048]{1,0:T(8,128)(2,1)} %get-tuple-element.8.refs_0_, bf16[64,512]{1,0:T(8,128)(2,1)} %get-tuple-element.9.refs_1_, bf16[64,512]{1,0:T(8,128)(2,1)} %get-tuple-element.10.refs_2_, ...), custom_call_target="tpu_custom_call" | custom-call | tf_op jit(solution)/shard_map/pallas_call | solution.py:410

commit v3 on v2

--- a/solution.py
+++ b/solution.py
@@ -14,7 +14,8 @@
 PER_KV = HQ // HK
 ROWS = 8
 HALO = 3
-TEAM = 8
+TEAM = 16
+PARTS = 2
 MESH = pl.DeviceIdType.MESH
 F32 = jnp.float32
 BF16 = jnp.bfloat16
@@ -38,8 +39,8 @@
     dq_hbm, dk_hbm, dv_hbm, dw_hbm,
     hid_ref, q_ref, k_ref, v_ref, o_ref, rows_ref, docs_ref, dq_ref, dk_ref, dw_ref,
     q32, o32, k32, v32, stage_s, came_s, stage_g, came_g, probs, acc_v, acc_k,
-    back_v, home_v, back, home, hid_out, hid_in, hid_t, gv, gv_in, term_out, term_in,
-    loaded, stored, sent, got,
+    back_v, home_v, back, home, hid_out, hid_in, hid_t, gv, gv_in, terms, term_out, term_in,
+    loaded, stored, sent, got, near, near_got,
 ):
     me = lax.axis_index("dp")
     tok = q_ref.shape[0]
@@ -47,6 +48,23 @@
     teams = n // TEAM
     member = lax.rem(me, TEAM)
     team = lax.div(me, TEAM)
+    core = lax.rem(me, 2)
+    spot = lax.rem(lax.div(me, 2), 4)
+    side = lax.rem(lax.div(me, 8), 2)
+
+    def place_in_team(a_core, a_side, a_spot):
+        return a_core * 8 + a_side * 4 + a_spot
+
+    def place_of(a_member):
+        return place_in_team(
+            lax.rem(a_member, 2), lax.div(a_member, 8), lax.rem(lax.div(a_member, 2), 4)
+        )
+
+    my_place = place_in_team(core, side, spot)
+
+    def device_at(a_core, a_side, a_spot):
+        return team * TEAM + a_side * 8 + a_spot * 2 + a_core
+
     group = lax.div(me, HK)
     scale = 1.0 / math.sqrt(DH)
     keys = n * 2 * ROWS
@@ -109,7 +127,7 @@
 
     def to_all(src, dst, index):
         def send(i, c):
-            peer = lax.rem(me + i * (TEAM + 1), n)
+            peer = lax.rem(me + i * 9, n)
             pltpu.make_async_remote_copy(
                 src.at[peer], dst.at[me], sent.at[index], got.at[index],
                 device_id=(peer,), device_id_type=MESH,
@@ -117,14 +135,6 @@
             return c
 
         lax.fori_loop(1, n, send, 0)
-
-    def to_team(src_of, dst, index):
-        for i in range(1, TEAM):
-            other = lax.rem(member + i, TEAM)
-            pltpu.make_async_remote_copy(
-                src_of(other), dst.at[member], sent.at[index], got.at[index],
-                device_id=(team * TEAM + other,), device_id_type=MESH,
-            ).start()
 
     lax.fori_loop(0, groups, packer(stage_s, q32, k32, True), 0)
     pl.semaphore_wait(barrier, n - 1)
@@ -148,8 +158,13 @@
                 ]
         else:
             hid_out[m] = hid_ref[:, m * span : (m + 1) * span]
-    to_team(lambda other: hid_out.at[other], hid_in, 1)
-    hid_in[member] = hid_out[member]
+    for i in range(1, TEAM):
+        other = lax.rem(member + i, TEAM)
+        pltpu.make_async_remote_copy(
+            hid_out.at[other], hid_in.at[my_place], sent.at[1], got.at[1],
+            device_id=(team * TEAM + other,), device_id_type=MESH,
+        ).start()
+    hid_in[my_place] = hid_out[member]
 
     came_s[me] = stage_s[me]
     came_g[me] = stage_g[me]
@@ -232,9 +247,6 @@
 
     lax.fori_loop(0, n // chunk, grads, 0)
     back[:, HEAD_ROWS:, :] = acc_k[...].reshape(n, 2 * ROWS, DH).astype(BF16)
-    to_all(back, home, 3)
-    home[me] = back[me]
-
     wait_bytes(hid_in, TEAM - 1, got.at[1])
     tile = DH // min(tok, DH)
     for t in range(TEAM * tok // DH):
@@ -260,26 +272,68 @@
         return c
 
     lax.fori_loop(0, groups // 2, place_v, 0)
-    to_team(lambda other: gv, gv_in, 4)
+
+    def pass_on(src, place, device, send_sem, recv_sem):
+        pltpu.make_async_remote_copy(
+            src, gv_in.at[place], send_sem, recv_sem,
+            device_id=(device,), device_id_type=MESH,
+        ).start()
+
+    partner_place = place_in_team(core, 1 - side, spot)
+    sibling = device_at(1 - core, side, spot)
+    pass_on(gv, my_place, device_at(core, 1 - side, spot), near.at[0], near_got.at[0])
+    for i in range(1, 4):
+        there = device_at(core, side, lax.rem(spot + i, 4))
+        pass_on(gv, my_place, there, near.at[i], near_got.at[i])
+    pass_on(gv, my_place, sibling, sent.at[4], got.at[4])
     store_v = pltpu.make_async_copy(gv, dv_hbm, stored.at[0])
     store_v.start()
-    gv_in[member] = gv[...]
-    wait_bytes(gv_in, TEAM - 1, got.at[4])
+    to_all(back, home, 3)
+    home[me] = back[me]
+    gv_in[my_place] = gv[...]
+
+    def landed(i):
+        pltpu.make_async_copy(gv, gv, near_got.at[i]).wait()
+
+    def across(place):
+        pass_on(gv_in.at[place], place, sibling, sent.at[4], got.at[4])
+
+    landed(0)
+    for i in range(1, 4):
+        there = device_at(core, side, lax.rem(spot + i, 4))
+        pass_on(gv_in.at[partner_place], partner_place, there, near.at[3 + i], near_got.at[3 + i])
+    across(partner_place)
+    for i in range(1, 4):
+        landed(i)
+        across(place_in_team(core, side, lax.rem(spot + 4 - i, 4)))
+    for i in range(1, 4):
+        landed(3 + i)
+        across(place_in_team(core, 1 - side, lax.rem(spot + 4 - i, 4)))
 
     grad_scale = 1.0 / math.sqrt(tok * n)
-
-    def term(p):
-        cols = hid_t[pl.ds(pl.multiple_of(p * width, width), width), :]
-        return dot(cols, gv_in[...].reshape(TEAM * tok, gv.shape[1]), 1, 0) * grad_scale
+    half = TEAM // 2 * tok
+
+    def half_term(p, which):
+        cols = hid_t[
+            pl.ds(pl.multiple_of(p * width, width), width),
+            pl.ds(pl.multiple_of(which * half, half), half),
+        ]
+        rows = gv_in[pl.ds(which * (TEAM // 2), TEAM // 2)].reshape(half, gv.shape[1])
+        return dot(cols, rows, 1, 0) * grad_scale
+
+    for i in range(teams):
+        other = lax.rem(team + i, teams)
+        terms[i] = half_term(other, core)
+    wait_bytes(gv_in, TEAM // 2, got.at[4])
 
     for i in range(1, teams):
         other = lax.rem(team + i, teams)
-        term_out[other] = term(other).astype(BF16)
+        term_out[other] = (terms[i] + half_term(other, 1 - core)).astype(BF16)
         pltpu.make_async_remote_copy(
             term_out.at[other], term_in.at[team], sent.at[5], got.at[5],
             device_id=(other * TEAM + member,), device_id_type=MESH,
         ).start()
-    dw_ref[...] = term(team)
+    dw_ref[...] = terms[0] + half_term(team, 1 - core)
 
     wait_bytes(home, n - 1, got.at[3])
 
@@ -318,7 +372,9 @@
     wait_bytes(hid_out, TEAM - 1, sent.at[1])
     wait_bytes(back_v, n - 1, sent.at[2])
     wait_bytes(back, n - 1, sent.at[3])
-    wait_bytes(gv_in, TEAM - 1, sent.at[4])
+    wait_bytes(gv_in, TEAM // 2, sent.at[4])
+    for i in range(7):
+        pltpu.make_async_copy(gv, gv, near.at[i]).wait()
     wait_bytes(term_out, teams - 1, sent.at[5])
     store_v.wait()
     store_q.wait()
@@ -327,17 +383,17 @@
 
 
 def hand_over(*refs):
-    count = (len(refs) - 2) // 3
-    srcs, dsts, held = refs[:count], refs[count : 2 * count], refs[2 * count : 3 * count]
-    in_sem, out_sem = refs[3 * count :]
-    ins = [pltpu.make_async_copy(srcs[i], held[i], in_sem.at[i]) for i in range(count)]
-    outs = [pltpu.make_async_copy(held[i], dsts[i], out_sem.at[i]) for i in range(count)]
-    for copy in ins:
+    count = len(refs) // 2
+    sems = refs[-1]
+    copies = []
+    for src, dst in zip(refs[:count], refs[count : 2 * count]):
+        rows = src.shape[0] // PARTS
+        for p in range(PARTS):
+            cut = pl.ds(p * rows, rows)
+            copies.append(pltpu.make_async_copy(src.at[cut], dst.at[cut], sems.at[len(copies)]))
+    for copy in copies:
         copy.start()
-    for i in range(count):
-        ins[i].wait()
-        outs[i].start()
-    for copy in outs:
+    for copy in copies:
         copy.wait()
 
 
@@ -396,10 +452,13 @@
             pltpu.VMEM((span, TEAM * tok), BF16),
             pltpu.VMEM((tok, kv), BF16),
             pltpu.VMEM((TEAM, tok, kv), BF16),
+            pltpu.VMEM((teams, width, kv), F32),
             pltpu.VMEM((teams, width, kv), BF16),
             pltpu.VMEM((teams, width, kv), BF16),
             pltpu.SemaphoreType.DMA((7,)),
             pltpu.SemaphoreType.DMA((4,)),
+            pltpu.SemaphoreType.DMA((7,)),
+            pltpu.SemaphoreType.DMA((7,)),
             pltpu.SemaphoreType.DMA((7,)),
             pltpu.SemaphoreType.DMA((7,)),
         ],
@@ -413,9 +472,7 @@
         in_specs=[whole] * 4,
         out_specs=(whole,) * 4,
         scratch_shapes=[
-            *(pltpu.VMEM(out.shape, out.dtype) for out in results),
-            pltpu.SemaphoreType.DMA((4,)),
-            pltpu.SemaphoreType.DMA((4,)),
+            pltpu.SemaphoreType.DMA((4 * PARTS,)),
         ],
         compiler_params=pltpu.CompilerParams(vmem_limit_bytes=62 * 2**20),
     )(*outs)

time: 56.8 us -> 76 us (1.34)
  Pallas kernels: 55.4 us -> 75.2 us
    pallas_call x1, Pallas kernels: 1.86 us -> 21 us  [local(): pl.pallas_call(hand_over, out_shape=results, in_specs=[whole] * 4, out_sp...]
where the time goes in v3:
time: 76 us; the launch traced here: 75.9 us
  Pallas kernels  75.2 us (99%)
    pallas_call x1, Pallas kernels, local(): pl.pallas_call(functools.partial(kernel, n, width), out_shape=results, in...  54.2 us
    pallas_call x1, Pallas kernels, local(): pl.pallas_call(hand_over, out_shape=results, in_specs=[whole] * 4, out_sp...  21 us

profile of v3, /device:TPU:0, one launch (start us, length us, event | category | flops | bytes accessed | tf_op | source)
XLA Modules:
  0.0 75.9 jit_solution(16295077129130160146)
XLA Ops:
  0.6 54.2 %shard_map.102 = (bf16[64,2048]{1,0:T(8,128)(2,1)}, bf16[64,512]{1,0:T(8,128)(2,1)}, bf16[64,512]{1,0:T(8,128)(2,1)}, f32[128,512]{1,0:T(8,128)}) custom-call(bf16[64,4096]{1,0:T(8,128)(2,1)} %hid_hbm.1, bf16[64,2048]{1,0:T(8,128)(2,1)} %q_hbm.1, bf16[64,512]{1,0:T(8,128)(2,1)} %k_hbm.1, bf16[64,512]{1,0:T(8,128)(2,1)} %v_hbm.1, bf16[64,2048]{1,0:T(8,128)(2,1)} %o_hbm.1, ...), custom_call_target="tpu_custom_call" | custom-call | tf_op jit(solution)/shard_map/pallas_call | solution.py:419
  54.8 21.0 %shard_map.103 = (bf16[64,2048]{1,0:T(8,128)(2,1)}, bf16[64,512]{1,0:T(8,128)(2,1)}, bf16[64,512]{1,0:T(8,128)(2,1)}, f32[128,512]{1,0:T(8,128)}) custom-call(bf16[64,2048]{1,0:T(8,128)(2,1)} %get-tuple-element.8.refs_0_, bf16[64,512]{1,0:T(8,128)(2,1)} %get-tuple-element.9.refs_1_, bf16[64,512]{1,0:T(8,128)(2,1)} %get-tuple-element.10.refs_2_, ...), custom_call_target="tpu_custom_call" | custom-call | tf_op jit(solution)/shard_map/pallas_call | solution.py:469

commit v4 on v3

--- a/solution.py
+++ b/solution.py
@@ -15,7 +15,7 @@
 ROWS = 8
 HALO = 3
 TEAM = 16
-PARTS = 2
+HALF = ROWS // 2
 MESH = pl.DeviceIdType.MESH
 F32 = jnp.float32
 BF16 = jnp.bfloat16
@@ -26,6 +26,19 @@
 
 def dot(a, b, da, db):
     return lax.dot_general(a, b, (((da,), (db,)), ((), ())), preferred_element_type=F32)
+
+
+def turn(x):
+    return pltpu.roll(x, HALF, x.ndim - 2)
+
+
+def low_line(x):
+    return lax.broadcasted_iota(jnp.int32, x.shape, x.ndim - 2) < HALF
+
+
+def halves_of(x, y):
+    low = low_line(x)
+    return jnp.where(low, x, turn(y)), jnp.where(low, turn(x), y)
 
 
 def wait_bytes(ref, count, sem):
@@ -38,7 +51,7 @@
     hid_hbm, q_hbm, k_hbm, v_hbm, o_hbm, rows_hbm, docs_hbm,
     dq_hbm, dk_hbm, dv_hbm, dw_hbm,
     hid_ref, q_ref, k_ref, v_ref, o_ref, rows_ref, docs_ref, dq_ref, dk_ref, dw_ref,
-    q32, o32, k32, v32, stage_s, came_s, stage_g, came_g, probs, acc_v, acc_k,
+    q32, o32, k32, v32, stage_s, came_s, stage_g, came_g, probs, k_rows, v_rows, acc_v, acc_k,
     back_v, home_v, back, home, hid_out, hid_in, hid_t, gv, gv_in, terms, term_out, term_in,
     loaded, stored, sent, got, near, near_got,
 ):
@@ -55,11 +68,6 @@
     def place_in_team(a_core, a_side, a_spot):
         return a_core * 8 + a_side * 4 + a_spot
 
-    def place_of(a_member):
-        return place_in_team(
-            lax.rem(a_member, 2), lax.div(a_member, 8), lax.rem(lax.div(a_member, 2), 4)
-        )
-
     my_place = place_in_team(core, side, spot)
 
     def device_at(a_core, a_side, a_spot):
@@ -67,9 +75,9 @@
 
     group = lax.div(me, HK)
     scale = 1.0 / math.sqrt(DH)
-    keys = n * 2 * ROWS
-    chunk = 8
-    q_rows = chunk * PER_KV * ROWS
+    keys = n * ROWS
+    chunk = 16
+    q_rows = chunk * HEAD_ROWS // 2
 
     loads = [
         pltpu.make_async_copy(src, dst, loaded.at[i])
@@ -114,10 +122,14 @@
         def pack(g, c):
             at = pl.multiple_of(g * ROWS, ROWS)
             for h in range(HK):
-                parts = [
-                    heads[pl.ds(at, ROWS), pl.ds((PER_KV * h + i) * DH, DH)]
-                    for i in range(PER_KV)
+                pairs = [
+                    halves_of(
+                        heads[pl.ds(at, ROWS), pl.ds((PER_KV * h + i) * DH, DH)],
+                        heads[pl.ds(at, ROWS), pl.ds((PER_KV * h + i + 1) * DH, DH)],
+                    )
+                    for i in range(0, PER_KV, 2)
                 ]
+                parts = [pair[b] for b in range(2) for pair in pairs]
                 part = tail[pl.ds(at, 2 * ROWS), pl.ds(h * DH, DH)]
                 parts.append(jnp.where(line == 0, doc_line, part) if with_docs else part)
                 dst[HK * g + h] = jnp.concatenate(parts, axis=0).astype(BF16)
@@ -139,13 +151,6 @@
     lax.fori_loop(0, groups, packer(stage_s, q32, k32, True), 0)
     pl.semaphore_wait(barrier, n - 1)
     to_all(stage_s, came_s, 0)
-
-    for load in loads[3:5]:
-        load.wait()
-    o32[...] = o_ref[...].astype(F32)
-    v32[ROWS:, :] = v_ref[...].astype(F32)
-    lax.fori_loop(0, groups, packer(stage_g, o32, v32, False), 0)
-    to_all(stage_g, came_g, 6)
 
     for load in loads[5:]:
         load.wait()
@@ -166,6 +171,13 @@
         ).start()
     hid_in[my_place] = hid_out[member]
 
+    for load in loads[3:5]:
+        load.wait()
+    o32[...] = o_ref[...].astype(F32)
+    v32[ROWS:, :] = v_ref[...].astype(F32)
+    lax.fori_loop(0, groups, packer(stage_g, o32, v32, False), 0)
+    to_all(stage_g, came_g, 6)
+
     came_s[me] = stage_s[me]
     came_g[me] = stage_g[me]
     acc_v[...] = jnp.zeros_like(acc_v)
@@ -189,64 +201,90 @@
     back_count = jnp.zeros((ROWS, 1), F32)
     for d in range(1, HALO + 1):
         back_count += jnp.where(docs[ROWS - d : 2 * ROWS - d] == own_docs, 1.0, 0.0)
-    first = (
-        lax.broadcasted_iota(jnp.int32, (ROWS, 1), 0) - back_count.astype(jnp.int32)
-    ) * n
-    first = jnp.broadcast_to(first[None], (q_rows // ROWS, ROWS, 1)).reshape(q_rows, 1)
+    first = jnp.broadcast_to(
+        (lax.broadcasted_iota(jnp.int32, (ROWS, 1), 0).astype(F32) - back_count) * n, (ROWS, DH)
+    )
+    firsts = [
+        jnp.broadcast_to(
+            part.astype(jnp.int32)[None, :, 0:1], (q_rows // ROWS, ROWS, 1)
+        ).reshape(q_rows, 1)
+        for part in halves_of(first, first)
+    ]
     col = lax.broadcasted_iota(jnp.int32, (1, keys), 1)
-    k_pos = (lax.rem(col, 2 * ROWS) - ROWS) * n + lax.div(col, 2 * ROWS)
+    k_pos = (lax.rem(col, ROWS) - HALF) * n + lax.div(col, ROWS)
     row = lax.broadcasted_iota(jnp.int32, (q_rows, 1), 0)
-    q_pos = lax.rem(row, ROWS) * n + lax.div(row, HEAD_ROWS)
-
-    def rows_of(ref, c):
-        return ref[pl.ds(c * chunk, chunk), 0:HEAD_ROWS, :].reshape(q_rows, DH)
-
-    def keys_of(ref):
-        return ref[:, HEAD_ROWS:, :].reshape(keys, DH)
-
-    def prob_of(c):
-        scores = dot(rows_of(came_s, c), keys_of(came_s), 1, 1) * scale
-        allowed = (k_pos >= first) & (k_pos <= q_pos + c * chunk)
+    q_pos = lax.rem(row, HALF) * n + lax.div(row, HEAD_ROWS // 2)
+
+    def spread(dst, src):
+        both = src[:, HEAD_ROWS:, :].astype(F32)
+        before, now = both[:, :ROWS], both[:, ROWS:]
+        mixed = turn(jnp.where(low_line(now), now, before))
+        dst[0] = mixed.reshape(keys, DH).astype(BF16)
+        dst[1] = now.reshape(keys, DH).astype(BF16)
+
+    def gathered(acc):
+        early = turn(acc[0].reshape(n, ROWS, DH))
+        late = acc[1].reshape(n, ROWS, DH)
+        low = low_line(late)
+        rows = [jnp.where(low, 0.0, early), jnp.where(low, early + late, late)]
+        return jnp.concatenate(rows, axis=1).astype(BF16)
+
+    def rows_of(ref, b, c):
+        cut = slice(b * HEAD_ROWS // 2, (b + 1) * HEAD_ROWS // 2)
+        return ref[pl.ds(c * chunk, chunk), cut, :].reshape(q_rows, DH)
+
+    def prob_of(b, c):
+        scores = dot(rows_of(came_s, b, c), k_rows[b], 1, 1)
+        pos = k_pos + b * HALF * n
+        allowed = (pos >= firsts[b]) & (pos <= q_pos + (c * chunk + b * HALF * n))
         scores = jnp.where(allowed, scores, -1000000000.0)
-        weights = jnp.exp(scores - jnp.max(scores, axis=1, keepdims=True))
+        top = jnp.max(scores, axis=1, keepdims=True)
+        weights = jnp.exp2((scores - top) * (scale * math.log2(math.e)))
         return weights * (1.0 / jnp.sum(weights, axis=1, keepdims=True))
 
-    kept = probs.shape[0] > q_rows
+    kept = probs.shape[1] > q_rows
 
     def prob_rows(c):
         return pl.ds(pl.multiple_of(c * q_rows, q_rows), q_rows)
 
     def soft(c, carry):
-        probs[prob_rows(c), :] = prob_of(c)
+        for b in range(2):
+            probs[b, prob_rows(c), :] = prob_of(b, c)
         return carry
 
+    spread(k_rows, came_s)
     if kept:
         lax.fori_loop(0, n // chunk, soft, 0)
 
     wait_bytes(came_g, n - 1, got.at[6])
 
     def value_grads(c, carry):
-        p = probs[prob_rows(c), :] if kept else prob_of(c)
-        acc_v[...] += dot(p.astype(BF16), rows_of(came_g, c), 0, 0)
+        for b in range(2):
+            p = probs[b, prob_rows(c), :] if kept else prob_of(b, c)
+            acc_v[b] += dot(p.astype(BF16), rows_of(came_g, b, c), 0, 0)
         return carry
 
     lax.fori_loop(0, n // chunk, value_grads, 0)
-    back_v[...] = acc_v[...].reshape(n, 2 * ROWS, DH).astype(BF16)
+    back_v[...] = gathered(acc_v)
     to_all(back_v, home_v, 2)
     home_v[me] = back_v[me]
+    spread(v_rows, came_g)
 
     def grads(c, carry):
-        p = probs[prob_rows(c), :] if kept else prob_of(c)
-        dprob = dot(rows_of(came_g, c), keys_of(came_g), 1, 1)
-        delta = jnp.sum(p * dprob, axis=1, keepdims=True)
-        dscore = (p * (dprob - delta) * scale).astype(BF16)
-        dq = dot(dscore, keys_of(came_s), 1, 0).astype(BF16)
-        back[pl.ds(c * chunk, chunk), 0:HEAD_ROWS, :] = dq.reshape(chunk, HEAD_ROWS, DH)
-        acc_k[...] += dot(dscore, rows_of(came_s, c), 0, 0)
+        for b in range(2):
+            p = probs[b, prob_rows(c), :] if kept else prob_of(b, c)
+            dprob = dot(rows_of(came_g, b, c), v_rows[b], 1, 1)
+            delta = jnp.sum(p * dprob, axis=1, keepdims=True)
+            dscore = (p * (dprob - delta) * scale).astype(BF16)
+            dq = dot(dscore, k_rows[b], 1, 0).astype(BF16)
+            cut = slice(b * HEAD_ROWS // 2, (b + 1) * HEAD_ROWS // 2)
+            back[pl.ds(c * chunk, chunk), cut, :] = dq.reshape(chunk, HEAD_ROWS // 2, DH)
+            acc_k[b] += dot(dscore, rows_of(came_s, b, c), 0, 0)
         return carry
 
     lax.fori_loop(0, n // chunk, grads, 0)
-    back[:, HEAD_ROWS:, :] = acc_k[...].reshape(n, 2 * ROWS, DH).astype(BF16)
+    back[:, HEAD_ROWS:, :] = gathered(acc_k)
+
     wait_bytes(hid_in, TEAM - 1, got.at[1])
     tile = DH // min(tok, DH)
     for t in range(TEAM * tok // DH):
@@ -346,11 +384,14 @@
             ).astype(BF16)
             lower = home[HK * 2 * pair + h, 0:HEAD_ROWS, :].astype(F32)
             upper = home[HK * (2 * pair + 1) + h, 0:HEAD_ROWS, :].astype(F32)
-            for i in range(PER_KV):
-                cut = slice(i * ROWS, (i + 1) * ROWS)
-                dq_ref[pl.ds(at, 2 * ROWS), pl.ds((PER_KV * h + i) * DH, DH)] = jnp.concatenate(
-                    [lower[cut], upper[cut]], axis=0
-                ).astype(BF16)
+            for i in range(0, PER_KV, 2):
+                a = slice(i * HALF, i * HALF + ROWS)
+                b = slice((PER_KV + i) * HALF, (PER_KV + i) * HALF + ROWS)
+                heads = zip(halves_of(lower[a], lower[b]), halves_of(upper[a], upper[b]))
+                for s, head in enumerate(heads):
+                    dq_ref[pl.ds(at, 2 * ROWS), pl.ds((PER_KV * h + i + s) * DH, DH)] = (
+                        jnp.concatenate(head, axis=0).astype(BF16)
+                    )
         return c
 
     lax.fori_loop(0, groups // 2, place, 0)
@@ -383,17 +424,17 @@
 
 
 def hand_over(*refs):
-    count = len(refs) // 2
-    sems = refs[-1]
-    copies = []
-    for src, dst in zip(refs[:count], refs[count : 2 * count]):
-        rows = src.shape[0] // PARTS
-        for p in range(PARTS):
-            cut = pl.ds(p * rows, rows)
-            copies.append(pltpu.make_async_copy(src.at[cut], dst.at[cut], sems.at[len(copies)]))
-    for copy in copies:
+    count = (len(refs) - 2) // 3
+    srcs, dsts, held = refs[:count], refs[count : 2 * count], refs[2 * count : 3 * count]
+    in_sem, out_sem = refs[3 * count :]
+    ins = [pltpu.make_async_copy(srcs[i], held[i], in_sem.at[i]) for i in range(count)]
+    outs = [pltpu.make_async_copy(held[i], dsts[i], out_sem.at[i]) for i in range(count)]
+    for copy in ins:
         copy.start()
-    for copy in copies:
+    for i in range(count):
+        ins[i].wait()
+        outs[i].start()
+    for copy in outs:
         copy.wait()
 
 
@@ -440,9 +481,11 @@
             pltpu.VMEM((n, MSG_ROWS, DH), BF16),
             pltpu.VMEM((n, MSG_ROWS, DH), BF16),
             pltpu.VMEM((n, MSG_ROWS, DH), BF16),
-            pltpu.VMEM((n * HEAD_ROWS if n <= 64 else ROWS, n * owned), F32),
-            pltpu.VMEM((n * owned, DH), F32),
-            pltpu.VMEM((n * owned, DH), F32),
+            pltpu.VMEM((2, n * HEAD_ROWS // 2 if n <= 64 else ROWS, n * ROWS), F32),
+            pltpu.VMEM((2, n * ROWS, DH), BF16),
+            pltpu.VMEM((2, n * ROWS, DH), BF16),
+            pltpu.VMEM((2, n * ROWS, DH), F32),
+            pltpu.VMEM((2, n * ROWS, DH), F32),
             pltpu.VMEM((n, owned, DH), BF16),
             pltpu.VMEM((n + HK, owned, DH), BF16),
             pltpu.VMEM((n, MSG_ROWS, DH), BF16),
@@ -472,7 +515,9 @@
         in_specs=[whole] * 4,
         out_specs=(whole,) * 4,
         scratch_shapes=[
-            pltpu.SemaphoreType.DMA((4 * PARTS,)),
+            *(pltpu.VMEM(out.shape, out.dtype) for out in results),
+            pltpu.SemaphoreType.DMA((4,)),
+            pltpu.SemaphoreType.DMA((4,)),
         ],
         compiler_params=pltpu.CompilerParams(vmem_limit_bytes=62 * 2**20),
     )(*outs)

time: 76 us -> 58.3 us (0.77)
  Pallas kernels: 75.2 us -> 57.5 us
    pallas_call x1, Pallas kernels: 21 us -> 1.86 us  [local(): pl.pallas_call(hand_over, out_shape=results, in_specs=[whole] * 4, out_sp...]
    pallas_call x1, Pallas kernels: 54.2 us -> 55.6 us  [local(): pl.pallas_call(functools.partial(kernel, n, width), out_shape=results, in...]
where the time goes in v4:
time: 58.3 us; the launch traced here: 58.1 us
  Pallas kernels  57.5 us (99%)
  between operations  0.64 us (1%)
    pallas_call x1, Pallas kernels, local(): pl.pallas_call(functools.partial(kernel, n, width), out_shape=results, in...  55.6 us
    pallas_call x1, Pallas kernels, local(): pl.pallas_call(hand_over, out_shape=results, in_specs=[whole] * 4, out_sp...  1.86 us

profile of v4, /device:TPU:0, one launch (start us, length us, event | category | flops | bytes accessed | tf_op | source)
XLA Modules:
  0.0 58.1 jit_solution(583943562716857590)
XLA Ops:
  0.6 55.6 %shard_map.102 = (bf16[64,2048]{1,0:T(8,128)(2,1)}, bf16[64,512]{1,0:T(8,128)(2,1)}, bf16[64,512]{1,0:T(8,128)(2,1)}, f32[128,512]{1,0:T(8,128)}) custom-call(bf16[64,4096]{1,0:T(8,128)(2,1)} %hid_hbm.1, bf16[64,2048]{1,0:T(8,128)(2,1)} %q_hbm.1, bf16[64,512]{1,0:T(8,128)(2,1)} %k_hbm.1, bf16[64,512]{1,0:T(8,128)(2,1)} %v_hbm.1, bf16[64,2048]{1,0:T(8,128)(2,1)} %o_hbm.1, ...), custom_call_target="tpu_custom_call" | custom-call | tf_op jit(solution)/shard_map/pallas_call | solution.py:460
  56.2 1.9 %shard_map.103 = (bf16[64,2048]{1,0:T(8,128)(2,1)}, bf16[64,512]{1,0:T(8,128)(2,1)}, bf16[64,512]{1,0:T(8,128)(2,1)}, f32[128,512]{1,0:T(8,128)}) custom-call(bf16[64,2048]{1,0:T(8,128)(2,1)} %get-tuple-element.8.refs_0_, bf16[64,512]{1,0:T(8,128)(2,1)} %get-tuple-element.9.refs_1_, bf16[64,512]{1,0:T(8,128)(2,1)} %get-tuple-element.10.refs_2_, ...), custom_call_target="tpu_custom_call" | custom-call | tf_op jit(solution)/shard_map/pallas_call | solution.py:512

commit v5 on v4

--- a/solution.py
+++ b/solution.py
@@ -51,7 +51,7 @@
     hid_hbm, q_hbm, k_hbm, v_hbm, o_hbm, rows_hbm, docs_hbm,
     dq_hbm, dk_hbm, dv_hbm, dw_hbm,
     hid_ref, q_ref, k_ref, v_ref, o_ref, rows_ref, docs_ref, dq_ref, dk_ref, dw_ref,
-    q32, o32, k32, v32, stage_s, came_s, stage_g, came_g, probs, k_rows, v_rows, acc_v, acc_k,
+    q32, o32, k32, v32, stage_s, came_s, stage_o, came_o, stage_v, came_v, probs, k_rows, v_rows, acc_v, acc_k,
     back_v, home_v, back, home, hid_out, hid_in, hid_t, gv, gv_in, terms, term_out, term_in,
     loaded, stored, sent, got, near, near_got,
 ):
@@ -118,7 +118,7 @@
     for j in range(docs_ref.shape[1]):
         doc_line = jnp.where(lane == j, (docs_ref[0, j] + 1).astype(F32), doc_line)
 
-    def packer(dst, heads, tail, with_docs):
+    def packer(dst, heads, tail):
         def pack(g, c):
             at = pl.multiple_of(g * ROWS, ROWS)
             for h in range(HK):
@@ -130,14 +130,15 @@
                     for i in range(0, PER_KV, 2)
                 ]
                 parts = [pair[b] for b in range(2) for pair in pairs]
-                part = tail[pl.ds(at, 2 * ROWS), pl.ds(h * DH, DH)]
-                parts.append(jnp.where(line == 0, doc_line, part) if with_docs else part)
+                if tail is not None:
+                    part = tail[pl.ds(at, 2 * ROWS), pl.ds(h * DH, DH)]
+                    parts.append(jnp.where(line == 0, doc_line, part))
                 dst[HK * g + h] = jnp.concatenate(parts, axis=0).astype(BF16)
             return c
 
         return pack
 
-    def to_all(src, dst, index):
+    def to_all(src, dst, index, begin=1, end=n):
         def send(i, c):
             peer = lax.rem(me + i * 9, n)
             pltpu.make_async_remote_copy(
@@ -146,11 +147,28 @@
             ).start()
             return c
 
-        lax.fori_loop(1, n, send, 0)
-
-    lax.fori_loop(0, groups, packer(stage_s, q32, k32, True), 0)
+        lax.fori_loop(begin, end, send, 0)
+
+    lax.fori_loop(0, groups, packer(stage_s, q32, k32), 0)
     pl.semaphore_wait(barrier, n - 1)
     to_all(stage_s, came_s, 0)
+
+    loads[3].wait()
+    o32[...] = o_ref[...].astype(F32)
+    lax.fori_loop(0, groups, packer(stage_o, o32, None), 0)
+    to_all(stage_o, came_o, 6)
+
+    loads[4].wait()
+    v32[ROWS:, :] = v_ref[...].astype(F32)
+
+    def pack_v(g, c):
+        at = pl.multiple_of(g * ROWS, ROWS)
+        for h in range(HK):
+            stage_v[HK * g + h] = v32[pl.ds(at, 2 * ROWS), pl.ds(h * DH, DH)].astype(BF16)
+        return c
+
+    lax.fori_loop(0, groups, pack_v, 0)
+    to_all(stage_v, came_v, 7)
 
     for load in loads[5:]:
         load.wait()
@@ -163,23 +181,9 @@
                 ]
         else:
             hid_out[m] = hid_ref[:, m * span : (m + 1) * span]
-    for i in range(1, TEAM):
-        other = lax.rem(member + i, TEAM)
-        pltpu.make_async_remote_copy(
-            hid_out.at[other], hid_in.at[my_place], sent.at[1], got.at[1],
-            device_id=(team * TEAM + other,), device_id_type=MESH,
-        ).start()
-    hid_in[my_place] = hid_out[member]
-
-    for load in loads[3:5]:
-        load.wait()
-    o32[...] = o_ref[...].astype(F32)
-    v32[ROWS:, :] = v_ref[...].astype(F32)
-    lax.fori_loop(0, groups, packer(stage_g, o32, v32, False), 0)
-    to_all(stage_g, came_g, 6)
-
     came_s[me] = stage_s[me]
-    came_g[me] = stage_g[me]
+    came_o[me] = stage_o[me]
+    came_v[me] = stage_v[me]
     acc_v[...] = jnp.zeros_like(acc_v)
     acc_k[...] = jnp.zeros_like(acc_k)
     home_v[n:, :, :] = jnp.zeros((HK, 2 * ROWS, DH), BF16)
@@ -216,7 +220,7 @@
     q_pos = lax.rem(row, HALF) * n + lax.div(row, HEAD_ROWS // 2)
 
     def spread(dst, src):
-        both = src[:, HEAD_ROWS:, :].astype(F32)
+        both = src.astype(F32)
         before, now = both[:, :ROWS], both[:, ROWS:]
         mixed = turn(jnp.where(low_line(now), now, before))
         dst[0] = mixed.reshape(keys, DH).astype(BF16)
@@ -252,28 +256,37 @@
             probs[b, prob_rows(c), :] = prob_of(b, c)
         return carry
 
-    spread(k_rows, came_s)
+    spread(k_rows, came_s[:, HEAD_ROWS:, :])
     if kept:
         lax.fori_loop(0, n // chunk, soft, 0)
 
-    wait_bytes(came_g, n - 1, got.at[6])
+    wait_bytes(came_o, n - 1, got.at[6])
 
     def value_grads(c, carry):
         for b in range(2):
             p = probs[b, prob_rows(c), :] if kept else prob_of(b, c)
-            acc_v[b] += dot(p.astype(BF16), rows_of(came_g, b, c), 0, 0)
+            acc_v[b] += dot(p.astype(BF16), rows_of(came_o, b, c), 0, 0)
         return carry
 
     lax.fori_loop(0, n // chunk, value_grads, 0)
     back_v[...] = gathered(acc_v)
     to_all(back_v, home_v, 2)
     home_v[me] = back_v[me]
-    spread(v_rows, came_g)
+    for i in range(1, TEAM):
+        other = lax.rem(member + i, TEAM)
+        pltpu.make_async_remote_copy(
+            hid_out.at[other], hid_in.at[my_place], sent.at[1], got.at[1],
+            device_id=(team * TEAM + other,), device_id_type=MESH,
+        ).start()
+    hid_in[my_place] = hid_out[member]
+
+    wait_bytes(came_v, n - 1, got.at[7])
+    spread(v_rows, came_v[...])
 
     def grads(c, carry):
         for b in range(2):
             p = probs[b, prob_rows(c), :] if kept else prob_of(b, c)
-            dprob = dot(rows_of(came_g, b, c), v_rows[b], 1, 1)
+            dprob = dot(rows_of(came_o, b, c), v_rows[b], 1, 1)
             delta = jnp.sum(p * dprob, axis=1, keepdims=True)
             dscore = (p * (dprob - delta) * scale).astype(BF16)
             dq = dot(dscore, k_rows[b], 1, 0).astype(BF16)
@@ -284,16 +297,7 @@
 
     lax.fori_loop(0, n // chunk, grads, 0)
     back[:, HEAD_ROWS:, :] = gathered(acc_k)
-
-    wait_bytes(hid_in, TEAM - 1, got.at[1])
-    tile = DH // min(tok, DH)
-    for t in range(TEAM * tok // DH):
-        if tile > 1:
-            rows = hid_in[t * tile : (t + 1) * tile].reshape(DH, span)
-        else:
-            per = tok // DH
-            rows = hid_in[t // per, (t % per) * DH : (t % per + 1) * DH, :]
-        hid_t[:, t * DH : (t + 1) * DH] = rows.T
+    to_all(back, home, 3, 1, n // 3)
 
     def summed(ref, g, h, at):
         own = ref[HK * g + h, at : at + 2 * ROWS, :].astype(F32)
@@ -326,7 +330,7 @@
     pass_on(gv, my_place, sibling, sent.at[4], got.at[4])
     store_v = pltpu.make_async_copy(gv, dv_hbm, stored.at[0])
     store_v.start()
-    to_all(back, home, 3)
+    to_all(back, home, 3, n // 3, n)
     home[me] = back[me]
     gv_in[my_place] = gv[...]
 
@@ -347,6 +351,16 @@
     for i in range(1, 4):
         landed(3 + i)
         across(place_in_team(core, 1 - side, lax.rem(spot + 4 - i, 4)))
+
+    wait_bytes(hid_in, TEAM - 1, got.at[1])
+    tile = DH // min(tok, DH)
+    for t in range(TEAM * tok // DH):
+        if tile > 1:
+            rows = hid_in[t * tile : (t + 1) * tile].reshape(DH, span)
+        else:
+            per = tok // DH
+            rows = hid_in[t // per, (t % per) * DH : (t % per + 1) * DH, :]
+        hid_t[:, t * DH : (t + 1) * DH] = rows.T
 
     grad_scale = 1.0 / math.sqrt(tok * n)
     half = TEAM // 2 * tok
@@ -409,7 +423,8 @@
     store_w.start()
 
     wait_bytes(stage_s, n - 1, sent.at[0])
-    wait_bytes(stage_g, n - 1, sent.at[6])
+    wait_bytes(stage_o, n - 1, sent.at[6])
+    wait_bytes(stage_v, n - 1, sent.at[7])
     wait_bytes(hid_out, TEAM - 1, sent.at[1])
     wait_bytes(back_v, n - 1, sent.at[2])
     wait_bytes(back, n - 1, sent.at[3])
@@ -479,8 +494,10 @@
             pltpu.VMEM((tok + ROWS, kv), F32),
             pltpu.VMEM((n, MSG_ROWS, DH), BF16),
             pltpu.VMEM((n, MSG_ROWS, DH), BF16),
-            pltpu.VMEM((n, MSG_ROWS, DH), BF16),
-            pltpu.VMEM((n, MSG_ROWS, DH), BF16),
+            pltpu.VMEM((n, HEAD_ROWS, DH), BF16),
+            pltpu.VMEM((n, HEAD_ROWS, DH), BF16),
+            pltpu.VMEM((n, owned, DH), BF16),
+            pltpu.VMEM((n, owned, DH), BF16),
             pltpu.VMEM((2, n * HEAD_ROWS // 2 if n <= 64 else ROWS, n * ROWS), F32),
             pltpu.VMEM((2, n * ROWS, DH), BF16),
             pltpu.VMEM((2, n * ROWS, DH), BF16),
@@ -500,8 +517,8 @@
             pltpu.VMEM((teams, width, kv), BF16),
             pltpu.SemaphoreType.DMA((7,)),
             pltpu.SemaphoreType.DMA((4,)),
-            pltpu.SemaphoreType.DMA((7,)),
-            pltpu.SemaphoreType.DMA((7,)),
+            pltpu.SemaphoreType.DMA((8,)),
+            pltpu.SemaphoreType.DMA((8,)),
             pltpu.SemaphoreType.DMA((7,)),
             pltpu.SemaphoreType.DMA((7,)),
         ],

time: 58.3 us -> 57.4 us (0.985)
  Pallas kernels: 57.5 us -> 56.6 us
    pallas_call x1, Pallas kernels: 55.6 us -> 54.7 us  [local(): pl.pallas_call(functools.partial(kernel, n, width), out_shape=results, in...]
where the time goes in v5:
time: 57.4 us; the launch traced here: 57.2 us
  Pallas kernels  56.6 us (99%)
  between operations  0.64 us (1%)
    pallas_call x1, Pallas kernels, local(): pl.pallas_call(functools.partial(kernel, n, width), out_shape=results, in...  54.7 us
    pallas_call x1, Pallas kernels, local(): pl.pallas_call(hand_over, out_shape=results, in_specs=[whole] * 4, out_sp...  1.86 us

profile of v5, /device:TPU:0, one launch (start us, length us, event | category | flops | bytes accessed | tf_op | source)
XLA Modules:
  0.0 57.2 jit_solution(2631319548214278100)
XLA Ops:
  0.6 54.7 %shard_map.102 = (bf16[64,2048]{1,0:T(8,128)(2,1)}, bf16[64,512]{1,0:T(8,128)(2,1)}, bf16[64,512]{1,0:T(8,128)(2,1)}, f32[128,512]{1,0:T(8,128)}) custom-call(bf16[64,4096]{1,0:T(8,128)(2,1)} %hid_hbm.1, bf16[64,2048]{1,0:T(8,128)(2,1)} %q_hbm.1, bf16[64,512]{1,0:T(8,128)(2,1)} %k_hbm.1, bf16[64,512]{1,0:T(8,128)(2,1)} %v_hbm.1, bf16[64,2048]{1,0:T(8,128)(2,1)} %o_hbm.1, ...), custom_call_target="tpu_custom_call" | custom-call | tf_op jit(solution)/shard_map/pallas_call | solution.py:475
  55.3 1.9 %shard_map.103 = (bf16[64,2048]{1,0:T(8,128)(2,1)}, bf16[64,512]{1,0:T(8,128)(2,1)}, bf16[64,512]{1,0:T(8,128)(2,1)}, f32[128,512]{1,0:T(8,128)}) custom-call(bf16[64,2048]{1,0:T(8,128)(2,1)} %get-tuple-element.8.refs_0_, bf16[64,512]{1,0:T(8,128)(2,1)} %get-tuple-element.9.refs_1_, bf16[64,512]{1,0:T(8,128)(2,1)} %get-tuple-element.10.refs_2_, ...), custom_call_target="tpu_custom_call" | custom-call | tf_op jit(solution)/shard_map/pallas_call | solution.py:529

commit v6 on v5

--- a/solution.py
+++ b/solution.py
@@ -51,7 +51,7 @@
     hid_hbm, q_hbm, k_hbm, v_hbm, o_hbm, rows_hbm, docs_hbm,
     dq_hbm, dk_hbm, dv_hbm, dw_hbm,
     hid_ref, q_ref, k_ref, v_ref, o_ref, rows_ref, docs_ref, dq_ref, dk_ref, dw_ref,
-    q32, o32, k32, v32, stage_s, came_s, stage_o, came_o, stage_v, came_v, probs, k_rows, v_rows, acc_v, acc_k,
+    q32, o32, k32, v32, stage_s, came_s, stage_o, came_o, stage_v, came_v, probs, probs_t, k_rows, v_rows, acc_v, acc_k,
     back_v, home_v, back, home, hid_out, hid_in, hid_t, gv, gv_in, terms, term_out, term_in,
     loaded, stored, sent, got, near, near_got,
 ):
@@ -184,7 +184,6 @@
     came_s[me] = stage_s[me]
     came_o[me] = stage_o[me]
     came_v[me] = stage_v[me]
-    acc_v[...] = jnp.zeros_like(acc_v)
     acc_k[...] = jnp.zeros_like(acc_k)
     home_v[n:, :, :] = jnp.zeros((HK, 2 * ROWS, DH), BF16)
     home[n:, :, :] = jnp.zeros((HK, MSG_ROWS, DH), BF16)
@@ -253,22 +252,20 @@
 
     def soft(c, carry):
         for b in range(2):
-            probs[b, prob_rows(c), :] = prob_of(b, c)
+            p = prob_of(b, c)
+            if kept:
+                probs[b, prob_rows(c), :] = p
+            probs_t[b, :, prob_rows(c)] = p.astype(BF16).T
         return carry
 
     spread(k_rows, came_s[:, HEAD_ROWS:, :])
-    if kept:
-        lax.fori_loop(0, n // chunk, soft, 0)
+    lax.fori_loop(0, n // chunk, soft, 0)
 
     wait_bytes(came_o, n - 1, got.at[6])
 
-    def value_grads(c, carry):
-        for b in range(2):
-            p = probs[b, prob_rows(c), :] if kept else prob_of(b, c)
-            acc_v[b] += dot(p.astype(BF16), rows_of(came_o, b, c), 0, 0)
-        return carry
-
-    lax.fori_loop(0, n // chunk, value_grads, 0)
+    for b in range(2):
+        cut = slice(b * HEAD_ROWS // 2, (b + 1) * HEAD_ROWS // 2)
+        acc_v[b] = dot(probs_t[b], came_o[:, cut, :].reshape(n * HEAD_ROWS // 2, DH), 1, 0)
     back_v[...] = gathered(acc_v)
     to_all(back_v, home_v, 2)
     home_v[me] = back_v[me]
@@ -297,7 +294,7 @@
 
     lax.fori_loop(0, n // chunk, grads, 0)
     back[:, HEAD_ROWS:, :] = gathered(acc_k)
-    to_all(back, home, 3, 1, n // 3)
+    to_all(back, home, 3, 1, n // 4)
 
     def summed(ref, g, h, at):
         own = ref[HK * g + h, at : at + 2 * ROWS, :].astype(F32)
@@ -321,36 +318,24 @@
             device_id=(device,), device_id_type=MESH,
         ).start()
 
-    partner_place = place_in_team(core, 1 - side, spot)
     sibling = device_at(1 - core, side, spot)
-    pass_on(gv, my_place, device_at(core, 1 - side, spot), near.at[0], near_got.at[0])
-    for i in range(1, 4):
-        there = device_at(core, side, lax.rem(spot + i, 4))
-        pass_on(gv, my_place, there, near.at[i], near_got.at[i])
+    chip = side * 4 + spot
+    order = (4, 1, 7, 3, 5, 2, 6)
+    for j in order:
+        there = lax.rem(chip + j, 8)
+        device = device_at(core, lax.div(there, 4), lax.rem(there, 4))
+        pass_on(gv, my_place, device, near.at[j - 1], near_got.at[j - 1])
     pass_on(gv, my_place, sibling, sent.at[4], got.at[4])
     store_v = pltpu.make_async_copy(gv, dv_hbm, stored.at[0])
     store_v.start()
-    to_all(back, home, 3, n // 3, n)
+    to_all(back, home, 3, n // 4, n)
     home[me] = back[me]
     gv_in[my_place] = gv[...]
 
-    def landed(i):
-        pltpu.make_async_copy(gv, gv, near_got.at[i]).wait()
-
-    def across(place):
+    for j in order:
+        pltpu.make_async_copy(gv, gv, near_got.at[j - 1]).wait()
+        place = core * 8 + lax.rem(chip + 8 - j, 8)
         pass_on(gv_in.at[place], place, sibling, sent.at[4], got.at[4])
-
-    landed(0)
-    for i in range(1, 4):
-        there = device_at(core, side, lax.rem(spot + i, 4))
-        pass_on(gv_in.at[partner_place], partner_place, there, near.at[3 + i], near_got.at[3 + i])
-    across(partner_place)
-    for i in range(1, 4):
-        landed(i)
-        across(place_in_team(core, side, lax.rem(spot + 4 - i, 4)))
-    for i in range(1, 4):
-        landed(3 + i)
-        across(place_in_team(core, 1 - side, lax.rem(spot + 4 - i, 4)))
 
     wait_bytes(hid_in, TEAM - 1, got.at[1])
     tile = DH // min(tok, DH)
@@ -499,6 +484,7 @@
             pltpu.VMEM((n, owned, DH), BF16),
             pltpu.VMEM((n, owned, DH), BF16),
             pltpu.VMEM((2, n * HEAD_ROWS // 2 if n <= 64 else ROWS, n * ROWS), F32),
+            pltpu.VMEM((2, n * ROWS, n * HEAD_ROWS // 2), BF16),
             pltpu.VMEM((2, n * ROWS, DH), BF16),
             pltpu.VMEM((2, n * ROWS, DH), BF16),
             pltpu.VMEM((2, n * ROWS, DH), F32),

time: 57.4 us -> 57 us (level)
  no operation moved by 1% of the time
where the time goes in v6:
time: 57 us; the launch traced here: 56.8 us
  Pallas kernels  56.2 us (99%)
  between operations  0.64 us (1%)
    pallas_call x1, Pallas kernels, local(): pl.pallas_call(functools.partial(kernel, n, width), out_shape=results, in...  54.3 us
    pallas_call x1, Pallas kernels, local(): pl.pallas_call(hand_over, out_shape=results, in_specs=[whole] * 4, out_sp...  1.86 us

profile of v6, /device:TPU:0, one launch (start us, length us, event | category | flops | bytes accessed | tf_op | source)
XLA Modules:
  0.0 56.8 jit_solution(16684806676074940909)
XLA Ops:
  0.6 54.3 %shard_map.102 = (bf16[64,2048]{1,0:T(8,128)(2,1)}, bf16[64,512]{1,0:T(8,128)(2,1)}, bf16[64,512]{1,0:T(8,128)(2,1)}, f32[128,512]{1,0:T(8,128)}) custom-call(bf16[64,4096]{1,0:T(8,128)(2,1)} %hid_hbm.1, bf16[64,2048]{1,0:T(8,128)(2,1)} %q_hbm.1, bf16[64,512]{1,0:T(8,128)(2,1)} %k_hbm.1, bf16[64,512]{1,0:T(8,128)(2,1)} %v_hbm.1, bf16[64,2048]{1,0:T(8,128)(2,1)} %o_hbm.1, ...), custom_call_target="tpu_custom_call" | custom-call | tf_op jit(solution)/shard_map/pallas_call | solution.py:460
  55.0 1.9 %shard_map.103 = (bf16[64,2048]{1,0:T(8,128)(2,1)}, bf16[64,512]{1,0:T(8,128)(2,1)}, bf16[64,512]{1,0:T(8,128)(2,1)}, f32[128,512]{1,0:T(8,128)}) custom-call(bf16[64,2048]{1,0:T(8,128)(2,1)} %get-tuple-element.8.refs_0_, bf16[64,512]{1,0:T(8,128)(2,1)} %get-tuple-element.9.refs_1_, bf16[64,512]{1,0:T(8,128)(2,1)} %get-tuple-element.10.refs_2_, ...), custom_call_target="tpu_custom_call" | custom-call | tf_op jit(solution)/shard_map/pallas_call | solution.py:515

commit v7 on v6

--- a/solution.py
+++ b/solution.py
@@ -181,6 +181,15 @@
                 ]
         else:
             hid_out[m] = hid_ref[:, m * span : (m + 1) * span]
+    for i in range(1, TEAM):
+        other = lax.rem(member + i, TEAM)
+        pltpu.make_async_remote_copy(
+            hid_out.at[other], hid_in.at[my_place], sent.at[1], got.at[1],
+            device_id=(team * TEAM + other,), device_id_type=MESH,
+        ).start()
+    hid_in[my_place] = hid_out[member]
+
+
     came_s[me] = stage_s[me]
     came_o[me] = stage_o[me]
     came_v[me] = stage_v[me]
@@ -269,14 +278,6 @@
     back_v[...] = gathered(acc_v)
     to_all(back_v, home_v, 2)
     home_v[me] = back_v[me]
-    for i in range(1, TEAM):
-        other = lax.rem(member + i, TEAM)
-        pltpu.make_async_remote_copy(
-            hid_out.at[other], hid_in.at[my_place], sent.at[1], got.at[1],
-            device_id=(team * TEAM + other,), device_id_type=MESH,
-        ).start()
-    hid_in[my_place] = hid_out[member]
-
     wait_bytes(came_v, n - 1, got.at[7])
     spread(v_rows, came_v[...])
 

time: 57 us -> 53.6 us (0.940)
  Pallas kernels: 56.2 us -> 52.8 us
    pallas_call x1, Pallas kernels: 54.3 us -> 50.9 us  [local(): pl.pallas_call(functools.partial(kernel, n, width), out_shape=results, in...]
where the time goes in v7:
time: 53.6 us; the launch traced here: 53.4 us
  Pallas kernels  52.8 us (99%)
  between operations  0.64 us (1%)
    pallas_call x1, Pallas kernels, local(): pl.pallas_call(functools.partial(kernel, n, width), out_shape=results, in...  50.9 us
    pallas_call x1, Pallas kernels, local(): pl.pallas_call(hand_over, out_shape=results, in_specs=[whole] * 4, out_sp...  1.86 us

profile of v7, /device:TPU:0, one launch (start us, length us, event | category | flops | bytes accessed | tf_op | source)
XLA Modules:
  0.0 53.4 jit_solution(1490876039041457600)
XLA Ops:
  0.6 50.9 %shard_map.102 = (bf16[64,2048]{1,0:T(8,128)(2,1)}, bf16[64,512]{1,0:T(8,128)(2,1)}, bf16[64,512]{1,0:T(8,128)(2,1)}, f32[128,512]{1,0:T(8,128)}) custom-call(bf16[64,4096]{1,0:T(8,128)(2,1)} %hid_hbm.1, bf16[64,2048]{1,0:T(8,128)(2,1)} %q_hbm.1, bf16[64,512]{1,0:T(8,128)(2,1)} %k_hbm.1, bf16[64,512]{1,0:T(8,128)(2,1)} %v_hbm.1, bf16[64,2048]{1,0:T(8,128)(2,1)} %o_hbm.1, ...), custom_call_target="tpu_custom_call" | custom-call | tf_op jit(solution)/shard_map/pallas_call | solution.py:461
  51.6 1.9 %shard_map.103 = (bf16[64,2048]{1,0:T(8,128)(2,1)}, bf16[64,512]{1,0:T(8,128)(2,1)}, bf16[64,512]{1,0:T(8,128)(2,1)}, f32[128,512]{1,0:T(8,128)}) custom-call(bf16[64,2048]{1,0:T(8,128)(2,1)} %get-tuple-element.8.refs_0_, bf16[64,512]{1,0:T(8,128)(2,1)} %get-tuple-element.9.refs_1_, bf16[64,512]{1,0:T(8,128)(2,1)} %get-tuple-element.10.refs_2_, ...), custom_call_target="tpu_custom_call" | custom-call | tf_op jit(solution)/shard_map/pallas_call | solution.py:516
